TPU v7x, 32 devices: a whole 2x2x4 slice. The times are simulated.
32 devices in a mesh: dp: 4 (over z), pipe: 4 (over y, x), tensor: 2 (over core).
Axes of the slice: x: 2, y: 2, z: 4, core: 2. Of those that a mesh axis runs over, the one named last changes fastest.
Arguments:
- embeds: bfloat16 [16, 64, 4096], P('dp', 'tensor'), parts along dimension 0, may hold values from -6 to 6
- labels: int32 [16, 64], P('dp'), parts along dimension 0, may hold values from 0 to 6143
- norm_gain: float32 [4, 4096], P('pipe'), may hold values from 0.5 to 1.5
- w_query: bfloat16 [4, 4096, 2048], P('pipe', None, 'tensor'), may hold values from -0.09375 to 0.09375
- w_key: bfloat16 [4, 4096, 1024], P('pipe', None, 'tensor'), may hold values from -0.09375 to 0.09375
- w_value: bfloat16 [4, 4096, 1024], P('pipe', None, 'tensor'), may hold values from -0.09375 to 0.09375
- w_out: bfloat16 [4, 2048, 4096], P('pipe', 'tensor'), may hold values from -0.125 to 0.125
- final_gain: float32 [4096], replicated, may hold values from 0.5 to 1.5
- head_weight: bfloat16 [4096, 6144], P(None, ('pipe', 'tensor')), may hold values from -16 to 16
Outputs:
- token_loss: float32 [16, 64], P('dp', ('pipe', 'tensor')), parts along dimension 0
- scores: float32 [16], P('dp'), parts along dimension 0
There are 4 independent parts, one for each index of `dp`. A program takes and returns all parts, laid end to end along the dimension named above; an argument that names none is the same for every part. Nothing has to cross between parts.
All inputs are finite; a program needn't handle non-finite values.
Results may differ from a plain program's by a relative error of at most 0.014.
Values may be sent and summed in bfloat16 or wider, within the bound.
A program may use at most 128 MiB of HBM per device.

v0:
```python
import math

import jax
import jax.numpy as jnp
from jax import lax
from jax.sharding import PartitionSpec as P

HD = 128


EPSILON = 1e-05
ROPE_BASE = 500000.0


def passed_along(value, axis, by):
    size = lax.axis_size(axis)
    pairs = [(i, i + by) for i in range(size) if 0 <= i + by < size]
    return lax.ppermute(value, axis, pairs)


def broadcast(value, axis, source):
    kept = jnp.where(lax.axis_index(axis) == source, value, 0).astype(value.dtype)
    return lax.psum(kept, axis)


def normalize(states, gain_vec):
    values = states.astype(jnp.float32)
    return (
        values * lax.rsqrt(jnp.mean(values * values, axis=-1, keepdims=True) + EPSILON) * gain_vec
    )


def rotate(tensor, positions):
    half_dim = tensor.shape[-1] // 2
    index = jnp.arange(half_dim, dtype=jnp.float32)
    inverse = ROPE_BASE ** (-2.0 * index / tensor.shape[-1])
    angles = positions[:, None] * inverse[None, :]
    cosine = jnp.cos(angles)[:, None, :]
    sine = jnp.sin(angles)[:, None, :]
    first_half = tensor[..., :half_dim]
    second_half = tensor[..., half_dim:]
    return jnp.concatenate(
        [first_half * cosine - second_half * sine, second_half * cosine + first_half * sine],
        axis=-1,
    )


def project(segment, layer_query, layer_key, layer_value):
    n_rows = segment.shape[0]
    positions = jnp.arange(n_rows).astype(jnp.float32)
    query = jnp.dot(segment, layer_query, preferred_element_type=jnp.float32)
    query = rotate(query.reshape(n_rows, -1, HD), positions).reshape(n_rows, -1)
    keys = jnp.dot(segment, layer_key, preferred_element_type=jnp.float32)
    keys = rotate(keys.reshape(n_rows, -1, HD), positions).reshape(n_rows, -1)
    values = jnp.dot(segment, layer_value, preferred_element_type=jnp.float32)
    return jnp.concatenate([query, keys, values], axis=1)


def attend(projected, heads_q, heads_kv):
    n_rows = projected.shape[0]
    q_width = heads_q * HD
    k_width = heads_kv * HD
    query = projected[:, :q_width].reshape(n_rows, heads_kv, heads_q // heads_kv, HD)
    keys = projected[:, q_width : q_width + k_width].reshape(n_rows, heads_kv, HD)
    values = projected[:, q_width + k_width :].reshape(n_rows, heads_kv, HD)
    logits = jnp.einsum(
        "skgd,tkd->kgst", query, keys, preferred_element_type=jnp.float32
    ) / math.sqrt(HD)
    causal = jnp.arange(n_rows)[:, None] >= jnp.arange(n_rows)[None, :]
    weights_attn = jax.nn.softmax(jnp.where(causal, logits, -1e30), axis=-1).astype(jnp.bfloat16)
    context = jnp.einsum("kgst,tkd->skgd", weights_attn, values, preferred_element_type=jnp.float32)
    return context.astype(jnp.bfloat16).reshape(n_rows, q_width)


def per_device(embeds, labels, norm_gain, w_query, w_key, w_value, w_out, final_gain, head_weight):
    pipe_count = lax.axis_size("pipe")
    tensor_count = lax.axis_size("tensor")
    section_index = lax.axis_index("pipe")
    tensor_rank = lax.axis_index("tensor")
    layer_gain = norm_gain[0]
    layer_query = w_query[0]
    layer_key = w_key[0]
    layer_value = w_value[0]
    layer_out = w_out[0]
    heads_q = layer_query.shape[1] // HD
    heads_kv = layer_key.shape[1] // HD
    micro_count = embeds.shape[0]
    seq_len = embeds.shape[1] * tensor_count
    tick_count = micro_count + pipe_count - 1
    carried = jnp.zeros_like(embeds[0])
    finals = jnp.zeros_like(embeds)
    for step_index in range(tick_count):
        if step_index < micro_count:
            incoming = embeds[step_index]
        else:
            incoming = jnp.zeros_like(embeds[0])
        current = jnp.where(section_index == 0, incoming, carried)
        normed = normalize(current, layer_gain).astype(jnp.bfloat16)
        projected = project(
            lax.all_gather(normed, "tensor", axis=0, tiled=True),
            layer_query,
            layer_key,
            layer_value,
        ).astype(jnp.bfloat16)
        context = attend(projected, heads_q, heads_kv)
        block_out = lax.psum_scatter(
            jnp.dot(context, layer_out, preferred_element_type=jnp.float32).astype(jnp.bfloat16),
            "tensor",
            scatter_dimension=0,
            tiled=True,
        ).astype(jnp.float32)
        result = (current.astype(jnp.float32) + block_out).astype(jnp.bfloat16)
        finished = step_index - (pipe_count - 1)
        if finished >= 0:
            finals = finals.at[finished].set(result)
        if step_index + 1 < tick_count:
            carried = passed_along(result, "pipe", 1)
    hidden = normalize(finals, final_gain).astype(jnp.bfloat16)
    hidden = broadcast(hidden, "pipe", pipe_count - 1)
    hidden = lax.all_gather(hidden, "tensor", axis=1, tiled=True)
    model_width = hidden.shape[2]
    flat_rows = hidden.reshape(micro_count * seq_len, model_width)
    logits = jnp.dot(flat_rows, head_weight, preferred_element_type=jnp.float32)
    vocab_dev = head_weight.shape[1]
    device_slot = section_index * tensor_count + tensor_rank
    local_ids = labels.reshape(-1) - device_slot * vocab_dev
    onehot = local_ids[:, None] == jnp.arange(vocab_dev, dtype=jnp.int32)[None, :]
    target_local = jnp.sum(jnp.where(onehot, logits, 0.0), axis=-1)
    peak_local = jnp.max(logits, axis=-1)
    peak_row = lax.pmax(peak_local, ("pipe", "tensor"))
    exp_local = jnp.sum(jnp.exp(logits - peak_row[:, None]), axis=-1)
    exp_total, target = lax.psum((exp_local, target_local), ("pipe", "tensor"))
    log_norm = peak_row + jnp.log(exp_total)
    losses = (log_norm - target).reshape(micro_count, seq_len)
    errors = (jnp.exp(logits - log_norm[:, None]) - onehot.astype(jnp.float32)).astype(jnp.bfloat16)
    errors = errors.reshape(micro_count, seq_len, vocab_dev)
    gram_err = jnp.einsum("bsv,btv->bst", errors, errors, preferred_element_type=jnp.float32)
    gram_hid = jnp.einsum("bsd,btd->bst", hidden, hidden, preferred_element_type=jnp.float32)
    score_parts = jnp.sum(gram_err * gram_hid, axis=(1, 2))
    totals = lax.psum(score_parts, ("pipe", "tensor"))
    scores = jnp.sqrt(totals) / seq_len
    loss_width = seq_len // (pipe_count * tensor_count)
    token_loss = lax.dynamic_slice_in_dim(losses, device_slot * loss_width, loss_width, 1)
    return (token_loss, scores)


def solution(mesh):
    in_specs = (
        P("dp", "tensor", None),
        P("dp", None),
        P("pipe", None),
        P("pipe", None, "tensor"),
        P("pipe", None, "tensor"),
        P("pipe", None, "tensor"),
        P("pipe", "tensor", None),
        P(),
        P(None, ("pipe", "tensor")),
    )
    out_specs = (P("dp", ("pipe", "tensor")), P("dp"))
    return jax.shard_map(
        per_device, mesh=mesh, in_specs=in_specs, out_specs=out_specs, check_vma=False
    )
```

profile of v0, /device:TPU:0, one launch (start us, length us, event | category | flops | bytes accessed | tf_op | source)
XLA Modules:
  0.0 440.6 jit_solution(11859844831304183084)
XLA Ops:
  11.8 11.3 %copy.110 = bf16[1024,4096]{1,0:T(8,128)(2,1)} copy(bf16[1024,4096]{0,1:T(8,128)(2,1)} %bitcast.343) | data formatting | bytes 16777216 | tf_op jit(solution)/shard_map/dot_general | solution.py:51
  23.0 6.4 %copy.109 = bf16[512,4096]{1,0:T(8,128)(2,1)} copy(bf16[512,4096]{0,1:T(8,128)(2,1)} %bitcast.345) | data formatting | bytes 8388608 | tf_op jit(solution)/shard_map/dot_general | solution.py:53
  29.4 6.2 %fusion.169 = f32[64,8,128]{2,0,1:T(8,128)S(1)} fusion(bf16[8,128,4096]{2,1,0:T(8,128)(2,1)} %bitcast.329, bf16[64,4096]{1,0:T(8,128)(2,1)S(1)} %all_gather.24), kind=kOutput, calls=%fused_computation.183 | convolution fusion | flops 536870912 | bytes 9175040 | tf_op jit(solution)/shard_map/dot_general | solution.py:51
  41.8 5.9 %fusion.21 = bf16[64,4096]{1,0:T(8,128)(2,1)} fusion(bf16[64,1024]{1,0:T(8,128)(2,1)S(1)} %reshape.426, bf16[1,1024,4096]{2,1,0:T(8,128)(2,1)} %param.23), kind=kOutput, calls=%fused_computation.21 | convolution fusion | flops 537133056 | bytes 9043968 | tf_op jit(solution)/shard_map/dot_general | solution.py:107
  47.7 10.7 %reduce-scatter.8.cloned.1.call-done = bf16[32,4096]{1,0:T(8,128)(2,1)} async-done(((bf16[64,4096]{1,0:T(8,128)(2,1)}), bf16[32,4096]{1,0:T(8,128)(2,1)}) %reduce-scatter.8.cloned.1.call-update) | async-done | bytes 262160 | tf_op jit(solution)/shard_map/reduce_scatter | solution.py:106
  59.4 3.6 collective-permute-start
  63.1 6.0 %collective-permute-done = bf16[32,4096]{1,0:T(8,128)(2,1)S(1)} collective-permute-done((bf16[32,4096]{1,0:T(8,128)(2,1)S(1)}, bf16[32,4096]{1,0:T(8,128)(2,1)S(1)}, u32[]{:S(2)}, u32[]{:S(2)}) %collective-permute-start) | collective-permute-done | bytes 262176 | tf_op jit(solution)/shard_map/ppermute | solution.py:18
  71.8 3.6 fusion.167
  75.3 6.0 %fusion.165 = f32[64,8,128]{2,0,1:T(8,128)S(1)} fusion(bf16[8,128,4096]{2,1,0:T(8,128)(2,1)} %bitcast.330, bf16[64,4096]{1,0:T(8,128)(2,1)S(1)} %all_gather.25), kind=kOutput, calls=%fused_computation.179 | convolution fusion | flops 536870912 | bytes 9175040 | tf_op jit(solution)/shard_map/dot_general | solution.py:51
  85.9 5.8 %fusion.24 = bf16[64,4096]{1,0:T(8,128)(2,1)} fusion(bf16[64,1024]{1,0:T(8,128)(2,1)S(1)} %reshape.429, bf16[1,1024,4096]{2,1,0:T(8,128)(2,1)} %param.23), kind=kOutput, calls=%fused_computation.22 | convolution fusion | flops 537133056 | bytes 9043968 | tf_op jit(solution)/shard_map/dot_general | solution.py:107
  91.8 10.0 %reduce-scatter.10.cloned.1.call-done = bf16[32,4096]{1,0:T(8,128)(2,1)} async-done(((bf16[64,4096]{1,0:T(8,128)(2,1)}), bf16[32,4096]{1,0:T(8,128)(2,1)}) %reduce-scatter.10.cloned.1.call-update) | async-done | bytes 262160 | tf_op jit(solution)/shard_map/reduce_scatter | solution.py:106
  102.8 3.6 collective-permute-start.1
  106.4 6.0 %collective-permute-done.1 = bf16[32,4096]{1,0:T(8,128)(2,1)S(1)} collective-permute-done((bf16[32,4096]{1,0:T(8,128)(2,1)S(1)}, bf16[32,4096]{1,0:T(8,128)(2,1)S(1)}, u32[]{:S(2)}, u32[]{:S(2)}) %collective-permute-start.1) | collective-permute-done | bytes 262176 | tf_op jit(solution)/shard_map/ppermute | solution.py:18
  115.0 3.6 fusion.163
  118.5 6.0 %fusion.161 = f32[64,8,128]{2,0,1:T(8,128)S(1)} fusion(bf16[8,128,4096]{2,1,0:T(8,128)(2,1)} %bitcast.331, bf16[64,4096]{1,0:T(8,128)(2,1)S(1)} %all_gather.26), kind=kOutput, calls=%fused_computation.175 | convolution fusion | flops 536870912 | bytes 9175040 | tf_op jit(solution)/shard_map/dot_general | solution.py:51
  129.1 5.8 %fusion.27 = bf16[64,4096]{1,0:T(8,128)(2,1)} fusion(bf16[64,1024]{1,0:T(8,128)(2,1)S(1)} %reshape.432, bf16[1,1024,4096]{2,1,0:T(8,128)(2,1)} %param.23), kind=kOutput, calls=%fused_computation.23 | convolution fusion | flops 537133056 | bytes 9043968 | tf_op jit(solution)/shard_map/dot_general | solution.py:107
  135.0 10.0 %reduce-scatter.12.cloned.1.call-done = bf16[32,4096]{1,0:T(8,128)(2,1)} async-done(((bf16[64,4096]{1,0:T(8,128)(2,1)}), bf16[32,4096]{1,0:T(8,128)(2,1)}) %reduce-scatter.12.cloned.1.call-update) | async-done | bytes 262160 | tf_op jit(solution)/shard_map/reduce_scatter | solution.py:106
  146.0 3.6 collective-permute-start.2
  149.6 6.0 %collective-permute-done.2 = bf16[32,4096]{1,0:T(8,128)(2,1)S(1)} collective-permute-done((bf16[32,4096]{1,0:T(8,128)(2,1)S(1)}, bf16[32,4096]{1,0:T(8,128)(2,1)S(1)}, u32[]{:S(2)}, u32[]{:S(2)}) %collective-permute-start.2) | collective-permute-done | bytes 262176 | tf_op jit(solution)/shard_map/ppermute | solution.py:18
  158.4 3.6 fusion.159
  161.9 6.0 %fusion.157 = f32[64,8,128]{2,0,1:T(8,128)S(1)} fusion(bf16[8,128,4096]{2,1,0:T(8,128)(2,1)} %bitcast.332, bf16[64,4096]{1,0:T(8,128)(2,1)S(1)} %all_gather.27), kind=kOutput, calls=%fused_computation.171 | convolution fusion | flops 536870912 | bytes 9175040 | tf_op jit(solution)/shard_map/dot_general | solution.py:51
  169.0 3.0 fusion.103
  172.5 5.8 %fusion.30 = bf16[64,4096]{1,0:T(8,128)(2,1)} fusion(bf16[64,1024]{1,0:T(8,128)(2,1)S(1)} %reshape.435, bf16[1,1024,4096]{2,1,0:T(8,128)(2,1)} %param.23), kind=kOutput, calls=%fused_computation.24 | convolution fusion | flops 537133056 | bytes 9043968 | tf_op jit(solution)/shard_map/dot_general | solution.py:107
  178.4 10.0 %reduce-scatter.14.cloned.1.call-done = bf16[32,4096]{1,0:T(8,128)(2,1)} async-done(((bf16[64,4096]{1,0:T(8,128)(2,1)}), bf16[32,4096]{1,0:T(8,128)(2,1)}) %reduce-scatter.14.cloned.1.call-update) | async-done | bytes 262160 | tf_op jit(solution)/shard_map/reduce_scatter | solution.py:106
  189.4 3.6 collective-permute-start.3
  193.0 6.0 %collective-permute-done.3 = bf16[32,4096]{1,0:T(8,128)(2,1)S(1)} collective-permute-done((bf16[32,4096]{1,0:T(8,128)(2,1)S(1)}, bf16[32,4096]{1,0:T(8,128)(2,1)S(1)}, u32[]{:S(2)}, u32[]{:S(2)}) %collective-permute-start.3) | collective-permute-done | bytes 262176 | tf_op jit(solution)/shard_map/ppermute | solution.py:18
  201.5 3.6 fusion.155
  205.1 6.0 %fusion.153 = f32[64,8,128]{2,0,1:T(8,128)S(1)} fusion(bf16[8,128,4096]{2,1,0:T(8,128)(2,1)} %bitcast.333, bf16[64,4096]{1,0:T(8,128)(2,1)S(1)} %all_gather.28), kind=kOutput, calls=%fused_computation.167 | convolution fusion | flops 536870912 | bytes 9175040 | tf_op jit(solution)/shard_map/dot_general | solution.py:51
  215.7 5.8 %fusion.33 = bf16[64,4096]{1,0:T(8,128)(2,1)} fusion(bf16[64,1024]{1,0:T(8,128)(2,1)S(1)} %reshape.439, bf16[1,1024,4096]{2,1,0:T(8,128)(2,1)} %param.23), kind=kOutput, calls=%fused_computation.25 | convolution fusion | flops 537133056 | bytes 9043968 | tf_op jit(solution)/shard_map/dot_general | solution.py:107
  221.6 9.9 %reduce-scatter.16.cloned.1.call-done = bf16[32,4096]{1,0:T(8,128)(2,1)} async-done(((bf16[64,4096]{1,0:T(8,128)(2,1)}), bf16[32,4096]{1,0:T(8,128)(2,1)}) %reduce-scatter.16.cloned.1.call-update) | async-done | bytes 262160 | tf_op jit(solution)/shard_map/reduce_scatter | solution.py:106
  232.5 3.6 collective-permute-start.4
  236.2 6.0 %collective-permute-done.4 = bf16[32,4096]{1,0:T(8,128)(2,1)S(1)} collective-permute-done((bf16[32,4096]{1,0:T(8,128)(2,1)S(1)}, bf16[32,4096]{1,0:T(8,128)(2,1)S(1)}, u32[]{:S(2)}, u32[]{:S(2)}) %collective-permute-start.4) | collective-permute-done | bytes 262176 | tf_op jit(solution)/shard_map/ppermute | solution.py:18
  245.1 3.6 fusion.151
  248.7 6.0 %fusion.149 = f32[64,8,128]{2,0,1:T(8,128)S(1)} fusion(bf16[8,128,4096]{2,1,0:T(8,128)(2,1)} %bitcast.334, bf16[64,4096]{1,0:T(8,128)(2,1)S(1)} %all_gather.29), kind=kOutput, calls=%fused_computation.163 | convolution fusion | flops 536870912 | bytes 9175040 | tf_op jit(solution)/shard_map/dot_general | solution.py:51
  259.3 5.8 %fusion.36 = bf16[64,4096]{1,0:T(8,128)(2,1)} fusion(bf16[64,1024]{1,0:T(8,128)(2,1)S(1)} %reshape.443, bf16[1,1024,4096]{2,1,0:T(8,128)(2,1)} %param.23), kind=kOutput, calls=%fused_computation.26 | convolution fusion | flops 537133056 | bytes 9043968 | tf_op jit(solution)/shard_map/dot_general | solution.py:107
  265.1 10.0 %reduce-scatter.18.cloned.1.call-done = bf16[32,4096]{1,0:T(8,128)(2,1)} async-done(((bf16[64,4096]{1,0:T(8,128)(2,1)}), bf16[32,4096]{1,0:T(8,128)(2,1)}) %reduce-scatter.18.cloned.1.call-update) | async-done | bytes 262160 | tf_op jit(solution)/shard_map/reduce_scatter | solution.py:106
  276.2 3.6 collective-permute-start.5
  279.8 6.0 %collective-permute-done.5 = bf16[32,4096]{1,0:T(8,128)(2,1)S(1)} collective-permute-done((bf16[32,4096]{1,0:T(8,128)(2,1)S(1)}, bf16[32,4096]{1,0:T(8,128)(2,1)S(1)}, u32[]{:S(2)}, u32[]{:S(2)}) %collective-permute-start.5) | collective-permute-done | bytes 262176 | tf_op jit(solution)/shard_map/ppermute | solution.py:18
  288.3 3.6 fusion.147
  291.9 6.0 %fusion.145 = f32[64,8,128]{2,0,1:T(8,128)S(1)} fusion(bf16[8,128,4096]{2,1,0:T(8,128)(2,1)} %bitcast.335, bf16[64,4096]{1,0:T(8,128)(2,1)S(1)} %all_gather.30), kind=kOutput, calls=%fused_computation.159 | convolution fusion | flops 536870912 | bytes 9175040 | tf_op jit(solution)/shard_map/dot_general | solution.py:51
  302.5 5.7 %fusion.39 = bf16[64,4096]{1,0:T(8,128)(2,1)} fusion(bf16[64,1024]{1,0:T(8,128)(2,1)S(1)} %reshape.447, bf16[1,1024,4096]{2,1,0:T(8,128)(2,1)} %param.23), kind=kOutput, calls=%fused_computation.27 | convolution fusion | flops 537133056 | bytes 9043968 | tf_op jit(solution)/shard_map/dot_general | solution.py:107
  308.4 9.8 %reduce-scatter.20.cloned.1.call-done = bf16[32,4096]{1,0:T(8,128)(2,1)} async-done(((bf16[64,4096]{1,0:T(8,128)(2,1)}), bf16[32,4096]{1,0:T(8,128)(2,1)}) %reduce-scatter.20.cloned.1.call-update) | async-done | bytes 262160 | tf_op jit(solution)/shard_map/reduce_scatter | solution.py:106
  321.0 54.3 %all-reduce.4.cloned.1.call-done = bf16[4,32,4096]{2,1,0:T(8,128)(2,1)} async-done(((bf16[4,32,4096]{2,1,0:T(8,128)(2,1)}), bf16[4,32,4096]{2,1,0:T(8,128)(2,1)}) %all-reduce.4.cloned.1.call-update) | async-done | bytes 1048592 | tf_op jit(solution)/shard_map/psum | solution.py:23
  375.5 12.1 %all-gather.2.cloned.1.call-done = bf16[4,64,4096]{2,1,0:T(8,128)(2,1)} async-done(((bf16[4,32,4096]{2,1,0:T(8,128)(2,1)}), bf16[4,64,4096]{2,1,0:T(8,128)(2,1)}) %all-gather.2.cloned.1.call-update) | async-done | bytes 2097168 | tf_op jit(solution)/shard_map/all_gather | solution.py:120
  387.6 5.4 %fusion.254 = (f32[256]{0:T(256)S(1)}, f32[256,768]{1,0:T(8,128)S(1)}) fusion(bf16[256,4096]{1,0:T(8,128)(2,1)} %bitcast.344, bf16[4096,768]{1,0:T(8,128)(2,1)} %param.25), kind=kOutput, calls=%fused_computation.334 | convolution fusion | flops 1610809088 | bytes 9176064 | tf_op jit(solution)/shard_map/dot_general | solution.py:123
  393.0 14.3 %pmax.7 = f32[256]{0:T(256)S(1)} all-reduce(f32[256]{0:T(256)S(1)} %get-tuple-element.94), channel_id=1, replica_groups=mesh['dp'=4,'pipe'=4,'tensor'=2] {'pipe','tensor'}, use_global_device_ids=true, to_apply=%region_31.32 | all-reduce | flops 256 | bytes 2048 | tf_op jit(solution)/shard_map/pmax | solution.py:130
  407.8 11.8 %psum.29 = f32[256]{0:T(256)S(1)} all-reduce(f32[256]{0:T(256)S(1)} %get-tuple-element.51), channel_id=1, replica_groups=mesh['dp'=4,'pipe'=4,'tensor'=2] {'pipe','tensor'}, use_global_device_ids=true, to_apply=%region_33.34 | all-reduce | flops 256 | bytes 2048 | tf_op jit(solution)/shard_map/psum | solution.py:132
  420.9 11.8 %all-reduce.1 = (f32[256]{0:T(256)S(1)}, f32[4]{0:T(128)S(1)}) all-reduce(f32[256]{0:T(256)S(1)} %get-tuple-element.50, f32[4]{0:T(128)S(1)} %fusion.115), channel_id=1, replica_groups=mesh['dp'=4,'pipe'=4,'tensor'=2] {'pipe','tensor'}, use_global_device_ids=true, to_apply=%region_35.36 | all-reduce | flops 260 | bytes 2080 | tf_op jit(solution)/shard_map/psum | solution.py:132
  (154 shorter events, 62.9 us)
Async XLA Ops:
  7.2 51.2 %reduce-scatter.8.cloned.1.call-start = ((), (), s32[]{:S(2)}) async-start(), calls=%async_computation.7 | async-start | bytes 786432 | tf_op jit(solution)/shard_map/reduce_scatter | solution.py:106
  29.4 6.2 %copy-start = (bf16[512,4096]{1,0:T(8,128)(2,1)S(1)}, bf16[512,4096]{1,0:T(8,128)(2,1)}, u32[]{:S(2)}) copy-start(bf16[512,4096]{1,0:T(8,128)(2,1)} %copy.109) | copy-start | bytes 12582916
  41.7 16.6 %copy-start.2 = (bf16[4,32,4096]{2,1,0:T(8,128)(2,1)S(1)}, bf16[4,32,4096]{2,1,0:T(8,128)(2,1)}, u32[]{:S(2)}) copy-start(bf16[4,32,4096]{2,1,0:T(8,128)(2,1)} %param.17) | copy-start | bytes 3145732
  41.7 27.5 %copy-start.3 = (f32[1,4096]{1,0:T(1,128)S(1)}, f32[1,4096]{1,0:T(1,128)}, u32[]{:S(2)}) copy-start(f32[1,4096]{1,0:T(1,128)} %param.19) | copy-start | bytes 49156
  47.6 54.1 %reduce-scatter.10.cloned.1.call-start = ((), (), s32[]{:S(2)}) async-start(), calls=%async_computation.8 | async-start | bytes 786432 | tf_op jit(solution)/shard_map/reduce_scatter | solution.py:106
  59.4 9.6 %collective-permute-start = (bf16[32,4096]{1,0:T(8,128)(2,1)S(1)}, bf16[32,4096]{1,0:T(8,128)(2,1)S(1)}, u32[]{:S(2)}, u32[]{:S(2)}) collective-permute-start(bf16[32,4096]{1,0:T(8,128)(2,1)S(1)} %fusion.144), channel_id=1, source_target_pairs={{0,2},{2,4},{4,6},{1,3},{3,5},{5,7},{8,10},{10,12},{12,14},{9,11},... | collective-permute-start | bytes 786440 | tf_op jit(solution)/shard_map/ppermute | solution.py:18
  91.7 53.2 %reduce-scatter.12.cloned.1.call-start = ((), (), s32[]{:S(2)}) async-start(), calls=%async_computation.9 | async-start | bytes 786432 | tf_op jit(solution)/shard_map/reduce_scatter | solution.py:106
  102.8 9.6 %collective-permute-start.1 = (bf16[32,4096]{1,0:T(8,128)(2,1)S(1)}, bf16[32,4096]{1,0:T(8,128)(2,1)S(1)}, u32[]{:S(2)}, u32[]{:S(2)}) collective-permute-start(bf16[32,4096]{1,0:T(8,128)(2,1)S(1)} %fusion.120), channel_id=1, source_target_pairs={{0,2},{2,4},{4,6},{1,3},{3,5},{5,7},{8,10},{10,12},{12,14},{9,11},... | collective-permute-start | bytes 786440 | tf_op jit(solution)/shard_map/ppermute | solution.py:18
  134.9 53.5 %reduce-scatter.14.cloned.1.call-start = ((), (), s32[]{:S(2)}) async-start(), calls=%async_computation.10 | async-start | bytes 786432 | tf_op jit(solution)/shard_map/reduce_scatter | solution.py:106
  146.0 9.7 %collective-permute-start.2 = (bf16[32,4096]{1,0:T(8,128)(2,1)S(1)}, bf16[32,4096]{1,0:T(8,128)(2,1)S(1)}, u32[]{:S(2)}, u32[]{:S(2)}) collective-permute-start(bf16[32,4096]{1,0:T(8,128)(2,1)S(1)} %fusion.124), channel_id=1, source_target_pairs={{0,2},{2,4},{4,6},{1,3},{3,5},{5,7},{8,10},{10,12},{12,14},{9,11},... | collective-permute-start | bytes 786440 | tf_op jit(solution)/shard_map/ppermute | solution.py:18
  178.3 53.2 %reduce-scatter.16.cloned.1.call-start = ((), (), s32[]{:S(2)}) async-start(), calls=%async_computation.11 | async-start | bytes 786432 | tf_op jit(solution)/shard_map/reduce_scatter | solution.py:106
  189.4 9.6 %collective-permute-start.3 = (bf16[32,4096]{1,0:T(8,128)(2,1)S(1)}, bf16[32,4096]{1,0:T(8,128)(2,1)S(1)}, u32[]{:S(2)}, u32[]{:S(2)}) collective-permute-start(bf16[32,4096]{1,0:T(8,128)(2,1)S(1)} %fusion.128), channel_id=1, source_target_pairs={{0,2},{2,4},{4,6},{1,3},{3,5},{5,7},{8,10},{10,12},{12,14},{9,11},... | collective-permute-start | bytes 786440 | tf_op jit(solution)/shard_map/ppermute | solution.py:18
  221.5 53.6 %reduce-scatter.18.cloned.1.call-start = ((), (), s32[]{:S(2)}) async-start(), calls=%async_computation.12 | async-start | bytes 786432 | tf_op jit(solution)/shard_map/reduce_scatter | solution.py:106
  232.5 9.7 %collective-permute-start.4 = (bf16[32,4096]{1,0:T(8,128)(2,1)S(1)}, bf16[32,4096]{1,0:T(8,128)(2,1)S(1)}, u32[]{:S(2)}, u32[]{:S(2)}) collective-permute-start(bf16[32,4096]{1,0:T(8,128)(2,1)S(1)} %get-tuple-element.57), channel_id=1, source_target_pairs={{0,2},{2,4},{4,6},{1,3},{3,5},{5,7},{8,10},{10,12},{12,14},{9,11},... | collective-permute-start | bytes 786440 | tf_op jit(solution)/shard_map/ppermute | solution.py:18
  265.1 53.2 %reduce-scatter.20.cloned.1.call-start = ((), (), s32[]{:S(2)}) async-start(), calls=%async_computation.13 | async-start | bytes 786432 | tf_op jit(solution)/shard_map/reduce_scatter | solution.py:106
  276.2 9.6 %collective-permute-start.5 = (bf16[32,4096]{1,0:T(8,128)(2,1)S(1)}, bf16[32,4096]{1,0:T(8,128)(2,1)S(1)}, u32[]{:S(2)}, u32[]{:S(2)}) collective-permute-start(bf16[32,4096]{1,0:T(8,128)(2,1)S(1)} %get-tuple-element.55), channel_id=1, source_target_pairs={{0,2},{2,4},{4,6},{1,3},{3,5},{5,7},{8,10},{10,12},{12,14},{9,11},... | collective-permute-start | bytes 786440 | tf_op jit(solution)/shard_map/ppermute | solution.py:18
  302.4 17.2 %copy-start.4 = (f32[4096]{0:T(1024)S(1)}, f32[4096]{0:T(1024)}, u32[]{:S(2)}) copy-start(f32[4096]{0:T(1024)} %param.24) | copy-start | bytes 49156
  308.2 67.2 %copy-start.5 = (s32[4,64]{1,0:T(4,128)S(1)}, s32[4,64]{1,0:T(4,128)}, u32[]{:S(2)}) copy-start(s32[4,64]{1,0:T(4,128)} %param.18) | copy-start | bytes 3076
  308.2 67.2 %all-reduce.4.cloned.1.call-start = ((), (), s32[]{:S(2)}) async-start(), calls=%async_computation.14 | async-start | bytes 2097152 | tf_op jit(solution)/shard_map/psum | solution.py:23
  321.0 66.6 %all-gather.2.cloned.1.call-start = ((), (), s32[]{:S(2)}) async-start(), calls=%async_computation.15 | async-start | bytes 3145728 | tf_op jit(solution)/shard_map/all_gather | solution.py:120
  387.6 32.2 %copy-start.1 = (bf16[4,64,4096]{2,1,0:T(8,128)(2,1)S(1)}, bf16[4,64,4096]{2,1,0:T(8,128)(2,1)}, u32[]{:S(2)}) copy-start(bf16[4,64,4096]{2,1,0:T(8,128)(2,1)} %all-gather.2.cloned.1.call-done) | copy-start | bytes 6291460
Sparse Core Ops, SparseCore 0:
  47.8 10.5 reduce-scatter.7
  91.8 9.8 reduce-scatter.9
  135.0 9.8 reduce-scatter.11
  178.4 9.8 reduce-scatter.13
  221.6 9.8 reduce-scatter.15
  265.2 9.8 reduce-scatter.17
  308.3 9.8 reduce-scatter.19
  321.6 53.7 all-reduce.3
  377.0 10.5 all-gather.1
where the time goes:
time: 448 us; the launch traced here: 441 us
  waiting for transfers between devices  173 us (39%)
  matrix products  139 us (31%)
  blocking collectives  54 us (12%)
  starting transfers between devices  22.3 us (5%)
  local copies, waits for them, and re-layouts  20.2 us (5%)
  other arithmetic  17 us (4%)
  between operations  14.7 us (3%)
    reduce_scatter x7, waiting for transfers between devices, per_device(): lax.psum_scatter(jnp.dot(context, layer_out, preferred_element_type=jnp.f...  70.4 us
    psum x1, waiting for transfers between devices, broadcast(): return lax.psum(kept, axis)  54.3 us
    dot_general x7, matrix products, project(): query = jnp.dot(segment, layer_query, preferred_element_type=jnp.float32)  42.4 us
    dot_general x7, matrix products, per_device(): jnp.dot(context, layer_out, preferred_element_type=jnp.float32)  40.5 us
    ppermute x6, waiting for transfers between devices, passed_along(): return lax.ppermute(value, axis, pairs)  36 us
    psum x2, blocking collectives, per_device(): exp_total, target = lax.psum((exp_local, target_local), ('pipe', 'tensor'))  23.6 us
    dot_general x7, matrix products, project(): keys = jnp.dot(segment, layer_key, preferred_element_type=jnp.float32)  22.9 us
    ppermute x6, starting transfers between devices, passed_along(): return lax.ppermute(value, axis, pairs)  21.8 us
  transfers between devices with their start and end apart: 15, of which 15 were waited for; matrix products, arithmetic and copies ran while one was open for 0% of the time, Pallas kernels for 0%

commit v1 on v0

v1 whole, which is shorter than its diff:
```python
import functools
import math

import jax
import jax.numpy as jnp
import numpy as np
from jax import lax
from jax.experimental import pallas as pl
from jax.experimental.pallas import tpu as pltpu
from jax.sharding import PartitionSpec as P

HD = 128
EPSILON = 1e-05
ROPE_BASE = 500000.0
LANES = 128
MESH = pl.DeviceIdType.MESH
NEG = -1e30


def round_up(value, step):
    return (value + step - 1) // step * step


def rotary_tables(seq_len):
    half = HD // 2
    inverse = (ROPE_BASE ** (-2.0 * np.arange(half, dtype=np.float64) / HD)).astype(np.float32)
    angles = (np.arange(seq_len, dtype=np.float32)[:, None] * inverse[None, :]).astype(np.float64)
    cosine, sine = np.cos(angles), np.sin(angles)
    cos_full = np.concatenate([cosine, cosine], axis=1)
    sin_full = np.concatenate([-sine, sine], axis=1)
    cos_table = np.stack([cos_full, np.ones_like(cos_full)]).astype(np.float32)
    sin_table = np.stack([sin_full, np.zeros_like(sin_full)]).astype(np.float32)
    return cos_table, sin_table


def relay_kernel(
    dims,
    embeds_ref, labels_ref, gain_ref, w_query_ref, w_key_ref, w_value_ref, w_out_ref,
    final_gain_ref, head_ref, cos_ref, sin_ref,
    loss_ref, score_ref,
    wqkv, wout, whead, st_in, gat, flat, qkv, ctx, part, rs, outst, hid, logits, ghid,
    labcol, slab, stats, tots,
    w_sem, wo_sem, wh_sem, e_sem,
    in_send, in_recv, g_send, g_recv, r_send, r_recv,
    h_send, h_recv, s_send, s_recv, t_send, t_recv, u_send, u_recv,
):
    n_pipe, n_tensor, micro, rows, width, heads_q, heads_kv, vocab_dev = dims
    group = n_pipe * n_tensor
    seq_len = rows * n_tensor
    kv_width = heads_kv * HD
    per_kv = heads_q // heads_kv
    n_tiles = per_kv + 2
    n_out, _, out_width = wout.shape
    last = n_pipe - 1
    half = width // 2
    p = lax.axis_index("pipe")
    t = lax.axis_index("tensor")
    slot = p * n_tensor + t
    near = [n_pipe - 2, n_pipe - 3] if n_pipe >= 3 else list(range(last))
    far = [q for q in range(last) if q not in near]

    def w_copy(i):
        if i < per_kv:
            src = w_query_ref.at[0, :, pl.ds(i * kv_width, kv_width)]
        else:
            src = (w_key_ref if i == per_kv else w_value_ref).at[0]
        return pltpu.make_async_copy(src, wqkv.at[i], w_sem.at[i])

    def wo_copy(n):
        return pltpu.make_async_copy(
            w_out_ref.at[0, :, pl.ds(n * out_width, out_width)], wout.at[n], wo_sem.at[n]
        )

    def e_copy(m, n):
        return pltpu.make_async_copy(
            embeds_ref.at[m, :, pl.ds(n * out_width, out_width)], st_in.at[m, n], e_sem.at[m, n]
        )

    head_copy = pltpu.make_async_copy(head_ref, whead, wh_sem)

    @pl.when(p == 0)
    def _():
        for m in range(micro):
            for n in range(n_out):
                e_copy(m, n).start()

    for i in range(n_tiles):
        w_copy(i).start()
    for n in range(n_out):
        wo_copy(n).start()
    head_copy.start()

    def ring(j):
        peer = lax.rem(slot + j, group)
        return peer, {"pipe": peer // n_tensor, "tensor": lax.rem(peer, n_tensor)}

    barrier = pltpu.get_barrier_semaphore()
    for j in range(1, group):
        pl.semaphore_signal(barrier, inc=1, device_id=ring(j)[1], device_id_type=MESH)
    pl.semaphore_wait(barrier, group - 1)

    @pl.when(p == 0)
    def _():
        for m in range(micro):
            for n in range(n_out):
                e_copy(m, n).wait()

    def remote(src, dst, send, recv, device):
        return pltpu.make_async_remote_copy(
            src_ref=src, dst_ref=dst, send_sem=send, recv_sem=recv,
            device_id=device, device_id_type=MESH,
        )

    def mate(j):
        return lax.rem(t + j, n_tensor)

    def in_copy(m, n):
        return remote(outst.at[m, n], st_in.at[m, n], in_send.at[m, n], in_recv.at[m, n],
                      {"pipe": lax.rem(p + 1, n_pipe)})

    def g_copy(m, j):
        return remote(gat.at[m, t], gat.at[m, t], g_send.at[m, j], g_recv.at[m, t],
                      {"tensor": mate(j)})

    def g_arrival(m, j):
        who = mate(j)
        return remote(gat.at[m, who], gat.at[m, who], g_send.at[m, j], g_recv.at[m, who],
                      {"tensor": who})

    def r_copy(m, n, j):
        who = mate(j)
        return remote(part.at[m, n, who], rs.at[m, n, t], r_send.at[m, n, j],
                      r_recv.at[m, n, t], {"tensor": who})

    def r_arrival(m, n, j):
        who = mate(j)
        return remote(part.at[m, n, who], rs.at[m, n, who], r_send.at[m, n, j],
                      r_recv.at[m, n, who], {"tensor": who})

    def h_copy(m, h, k, to):
        piece = hid.at[m, t, :, pl.ds(h * half, half)]
        return remote(piece, piece, h_send.at[m, h, k], h_recv.at[m, h], {"pipe": to})

    def s_copy(m, j):
        return remote(hid.at[m, t], hid.at[m, t], s_send.at[m, j], s_recv.at[m, t],
                      {"tensor": mate(j)})

    def s_arrival(m, j):
        who = mate(j)
        return remote(hid.at[m, who], hid.at[m, who], s_send.at[m, j], s_recv.at[m, who],
                      {"tensor": who})

    def scaled(squares):
        return lax.rsqrt(squares * (1.0 / width) + EPSILON)

    row_at = lax.broadcasted_iota(jnp.int32, (per_kv * seq_len, seq_len), 0)
    key_at = lax.broadcasted_iota(jnp.int32, (per_kv * seq_len, seq_len), 1)
    causal = lax.rem(row_at, seq_len) >= key_at

    def layer(m, carry):
        @pl.when(p > 0)
        def _():
            for n in range(n_out):
                in_copy(m, n).wait_recv()

        squares = jnp.zeros((rows, 1), jnp.float32)
        for n in range(n_out):
            tile = st_in[m, n].astype(jnp.float32)
            squares += jnp.sum(tile * tile, axis=-1, keepdims=True)
        factor = scaled(squares)
        for n in range(n_out):
            cols = pl.ds(n * out_width, out_width)
            normed = st_in[m, n].astype(jnp.float32) * factor * gain_ref[:, cols]
            gat[m, t, :, cols] = normed.astype(jnp.bfloat16)
        for j in range(1, n_tensor):
            g_copy(m, j).start()
        for j in range(1, n_tensor):
            g_arrival(m, j).wait_recv()
        if rows % 16:
            flat[...] = gat[m].astype(jnp.float32).reshape(seq_len, width).astype(jnp.bfloat16)

        @pl.when(m == 0)
        def _():
            for i in range(n_tiles):
                w_copy(i).wait()

        def project(i, c):
            lhs = flat[...] if rows % 16 else gat[m].reshape(seq_len, width)
            product = jnp.dot(lhs, wqkv[i], preferred_element_type=jnp.float32)
            which = jnp.where(i == n_tiles - 1, 1, 0)
            cosine, sine = cos_ref[which], sin_ref[which]
            for h in range(heads_kv):
                one = product[:, h * HD : (h + 1) * HD]
                turned = one * cosine + pltpu.roll(one, HD // 2, 1) * sine
                qkv[i, :, h * HD : (h + 1) * HD] = turned.astype(jnp.bfloat16)
            return c

        lax.fori_loop(0, n_tiles, project, 0)

        for h in range(heads_kv):
            queries = []
            for g in range(per_kv):
                head = h * per_kv + g
                at = head % heads_kv * HD
                queries.append(qkv[head // heads_kv, :, at : at + HD])
            query = jnp.concatenate(queries, axis=0) if per_kv > 1 else queries[0]
            key = qkv[per_kv, :, h * HD : (h + 1) * HD]
            value = qkv[per_kv + 1, :, h * HD : (h + 1) * HD]
            scores = lax.dot_general(
                query, key, (((1,), (1,)), ((), ())), preferred_element_type=jnp.float32
            ) * (1.0 / math.sqrt(HD))
            scores = jnp.where(causal, scores, NEG)
            shifted = jnp.exp(scores - jnp.max(scores, axis=-1, keepdims=True))
            probs = (shifted / jnp.sum(shifted, axis=-1, keepdims=True)).astype(jnp.bfloat16)
            context = jnp.dot(probs, value, preferred_element_type=jnp.float32)
            for g in range(per_kv):
                at = (h * per_kv + g) * HD
                ctx[:, at : at + HD] = context[g * seq_len : (g + 1) * seq_len].astype(jnp.bfloat16)

        @pl.when(m == 0)
        def _():
            for n in range(n_out):
                wo_copy(n).wait()

        def output(n, c):
            product = jnp.dot(ctx[...], wout[n], preferred_element_type=jnp.float32)
            part[m, n] = product.reshape(n_tensor, rows, out_width).astype(jnp.bfloat16)
            for j in range(1, n_tensor):
                r_copy(m, n, j).start()
            return c

        lax.fori_loop(0, n_out, output, 0)

        def combine(n, total):
            block = part[m, n, t].astype(jnp.float32)
            for j in range(1, n_tensor):
                r_arrival(m, n, j).wait_recv()
                block += rs[m, n, mate(j)].astype(jnp.float32)
            state = (st_in[m, n].astype(jnp.float32) + block).astype(jnp.bfloat16)
            outst[m, n] = state

            @pl.when(p < last)
            def _():
                in_copy(m, n).start()

            wide = state.astype(jnp.float32)
            return total + jnp.sum(wide * wide, axis=-1, keepdims=True)

        total = lax.fori_loop(0, n_out, combine, jnp.zeros((rows, 1), jnp.float32))

        @pl.when(p == last)
        def _():
            last_factor = scaled(total)
            for n in range(n_out):
                cols = pl.ds(n * out_width, out_width)
                final = outst[m, n].astype(jnp.float32) * last_factor * final_gain_ref[:, cols]
                hid[m, t, :, cols] = final.astype(jnp.bfloat16)
            for step in range(2):
                for k, to in enumerate(near):
                    h_copy(m, (k + 1 + step) % 2, k, to).start()

        return carry

    lax.fori_loop(0, micro, layer, 0)

    pad = jnp.zeros((LANES - micro, seq_len), jnp.float32)
    labcol[...] = jnp.concatenate([labels_ref[...].astype(jnp.float32), pad], axis=0).T
    slab[...] = jnp.zeros_like(slab)
    lane = lax.broadcasted_iota(jnp.int32, (seq_len, LANES), 1)
    entry = (lax.broadcasted_iota(jnp.int32, (seq_len, vocab_dev), 1) + slot * vocab_dev).astype(
        jnp.float32
    )

    def onehot_of(m):
        own = jnp.sum(jnp.where(lane == m, labcol[...], 0.0), axis=-1, keepdims=True)
        return entry == own

    head_copy.wait()

    def head(m, carry):
        if len(near) == 2 and far:
            for k in range(2):
                first = (k + 1) % 2

                @pl.when(p == near[k])
                def _():
                    h_copy(m, first, 0, 0).wait_recv()
                    for f, to in enumerate(far):
                        h_copy(m, first, f, to).start()
                    h_copy(m, 1 - first, 0, 0).wait_recv()

            @pl.when(p < near[1])
            def _():
                for h in range(2):
                    h_copy(m, h, 0, last).wait_recv()
        else:
            @pl.when(p < last)
            def _():
                for h in range(2):
                    h_copy(m, h, 0, last).wait_recv()

        for j in range(1, n_tensor):
            s_copy(m, j).start()
        for j in range(1, n_tensor):
            s_arrival(m, j).wait_recv()
        if rows % 16:
            flat[...] = hid[m].astype(jnp.float32).reshape(seq_len, width).astype(jnp.bfloat16)
            lhs = flat[...]
        else:
            lhs = hid[m].reshape(seq_len, width)
        local = jnp.dot(lhs, whead[...], preferred_element_type=jnp.float32)
        logits[m] = local
        peak = jnp.max(local, axis=-1, keepdims=True)
        mass = jnp.sum(jnp.exp(local - peak), axis=-1, keepdims=True)
        target = jnp.sum(jnp.where(onehot_of(m), local, 0.0), axis=-1, keepdims=True)
        slab[...] = jnp.where(
            lane == m,
            peak,
            jnp.where(lane == micro + m, mass, jnp.where(lane == 2 * micro + m, target, slab[...])),
        )
        ghid[m] = lax.dot_general(
            lhs, lhs, (((1,), (1,)), ((), ())), preferred_element_type=jnp.float32
        )
        return carry

    lax.fori_loop(0, micro, head, 0)

    n_stats = stats.shape[1]
    stats[slot] = slab[...].T[:n_stats]

    def exchange(buffer, send, recv):
        def copy(j):
            peer, device = ring(j)
            return remote(buffer.at[slot], buffer.at[slot], send.at[j], recv.at[slot], device)

        def arrival(j):
            peer, device = ring(j)
            return remote(buffer.at[peer], buffer.at[peer], send.at[j], recv.at[peer], device)

        for j in range(1, group):
            copy(j).start()
        for j in range(1, group):
            arrival(j).wait_recv()
        return copy

    stats_copy = exchange(stats, t_send, t_recv)
    peaks = stats[:, :micro, :]
    peak_row = jnp.max(peaks, axis=0)
    masses = jnp.exp(peaks - peak_row[None]) * stats[:, micro : 2 * micro, :]
    log_norm = peak_row + jnp.log(jnp.sum(masses, axis=0))
    loss_ref[...] = log_norm - jnp.sum(stats[:, 2 * micro : 3 * micro, :], axis=0)
    labels_t = labcol[...]
    norm_t = jnp.concatenate([log_norm, pad], axis=0).T

    tot_rows = tots.shape[1]
    row_id = lax.broadcasted_iota(jnp.int32, (tot_rows, seq_len), 0)
    sums = jnp.zeros((tot_rows, seq_len), jnp.float32)
    for m in range(micro):
        onehot = (entry == labels_t[:, m : m + 1]).astype(jnp.float32)
        errors = (jnp.exp(logits[m] - norm_t[:, m : m + 1]) - onehot).astype(jnp.bfloat16)
        gram = lax.dot_general(
            errors, errors, (((1,), (1,)), ((), ())), preferred_element_type=jnp.float32
        )
        sums = jnp.where(row_id == m, jnp.sum(gram * ghid[m], axis=0, keepdims=True), sums)
    tots[slot] = sums
    tots_copy = exchange(tots, u_send, u_recv)
    total = jnp.sum(jnp.sum(tots[...], axis=0), axis=-1, keepdims=True)
    score_ref[...] = jnp.broadcast_to(jnp.sqrt(total) / seq_len, score_ref.shape)

    def drain(m, carry):
        for j in range(1, n_tensor):
            g_copy(m, j).wait_send()
            s_copy(m, j).wait_send()
            for n in range(n_out):
                r_copy(m, n, j).wait_send()

        @pl.when(p < last)
        def _():
            for n in range(n_out):
                in_copy(m, n).wait_send()

        @pl.when(p == last)
        def _():
            for h in range(2):
                for k, to in enumerate(near):
                    h_copy(m, h, k, to).wait_send()

        if len(near) == 2 and far:
            for k in range(2):
                first = (k + 1) % 2

                @pl.when(p == near[k])
                def _():
                    for f, to in enumerate(far):
                        h_copy(m, first, f, to).wait_send()

        return carry

    lax.fori_loop(0, micro, drain, 0)
    for j in range(1, group):
        stats_copy(j).wait_send()
        tots_copy(j).wait_send()


def per_device(embeds, labels, norm_gain, w_query, w_key, w_value, w_out, final_gain, head_weight):
    n_pipe = lax.axis_size("pipe")
    n_tensor = lax.axis_size("tensor")
    group = n_pipe * n_tensor
    micro, rows, width = embeds.shape
    seq_len = rows * n_tensor
    heads_q = w_query.shape[2] // HD
    heads_kv = w_key.shape[2] // HD
    kv_width = heads_kv * HD
    n_tiles = heads_q // heads_kv + 2
    depth = w_out.shape[1]
    vocab_dev = head_weight.shape[1]
    n_out = 4
    out_width = width // n_out
    n_far = max(n_pipe, 2)
    cos_table, sin_table = rotary_tables(seq_len)
    dims = (n_pipe, n_tensor, micro, rows, width, heads_q, heads_kv, vocab_dev)
    bf16, f32 = jnp.bfloat16, jnp.float32
    dma = pltpu.SemaphoreType.DMA
    any_spec = pl.BlockSpec(memory_space=pl.ANY)
    vmem_spec = pl.BlockSpec(memory_space=pltpu.VMEM)
    stat_rows = round_up(3 * micro, 8)
    tot_rows = round_up(micro, 8)
    losses, scores = pl.pallas_call(
        functools.partial(relay_kernel, dims),
        out_shape=(
            jax.ShapeDtypeStruct((micro, seq_len), f32),
            jax.ShapeDtypeStruct((tot_rows, LANES), f32),
        ),
        in_specs=[any_spec, vmem_spec, vmem_spec] + [any_spec] * 4
        + [vmem_spec, any_spec, vmem_spec, vmem_spec],
        out_specs=(vmem_spec, vmem_spec),
        scratch_shapes=[
            pltpu.VMEM((n_tiles, width, kv_width), bf16),
            pltpu.VMEM((n_out, depth, out_width), bf16),
            pltpu.VMEM((width, vocab_dev), bf16),
            pltpu.VMEM((micro, n_out, rows, out_width), bf16),
            pltpu.VMEM((micro, n_tensor, rows, width), bf16),
            pltpu.VMEM((seq_len, width) if rows % 16 else (16, LANES), bf16),
            pltpu.VMEM((n_tiles, seq_len, kv_width), bf16),
            pltpu.VMEM((seq_len, depth), bf16),
            pltpu.VMEM((micro, n_out, n_tensor, rows, out_width), bf16),
            pltpu.VMEM((micro, n_out, n_tensor, rows, out_width), bf16),
            pltpu.VMEM((micro, n_out, rows, out_width), bf16),
            pltpu.VMEM((micro, n_tensor, rows, width), bf16),
            pltpu.VMEM((micro, seq_len, vocab_dev), f32),
            pltpu.VMEM((micro, seq_len, seq_len), f32),
            pltpu.VMEM((seq_len, LANES), f32),
            pltpu.VMEM((seq_len, LANES), f32),
            pltpu.VMEM((group, stat_rows, seq_len), f32),
            pltpu.VMEM((group, tot_rows, seq_len), f32),
            dma((n_tiles,)), dma((n_out,)), dma, dma((micro, n_out)),
            dma((micro, n_out)), dma((micro, n_out)),
            dma((micro, n_tensor)), dma((micro, n_tensor)),
            dma((micro, n_out, n_tensor)), dma((micro, n_out, n_tensor)),
            dma((micro, 2, n_far)), dma((micro, 2)),
            dma((micro, n_tensor)), dma((micro, n_tensor)),
            dma((group,)), dma((group,)), dma((group,)), dma((group,)),
        ],
        compiler_params=pltpu.CompilerParams(
            collective_id=0, has_side_effects=True, vmem_limit_bytes=58 * 1024 * 1024
        ),
    )(
        embeds, labels, norm_gain, w_query, w_key, w_value, w_out,
        final_gain.reshape(1, width), head_weight, jnp.asarray(cos_table), jnp.asarray(sin_table),
    )
    loss_width = seq_len // group
    device_slot = lax.axis_index("pipe") * n_tensor + lax.axis_index("tensor")
    token_loss = lax.dynamic_slice_in_dim(losses, device_slot * loss_width, loss_width, 1)
    return (token_loss, scores[:micro, 0])


def solution(mesh):
    in_specs = (
        P("dp", "tensor", None),
        P("dp", None),
        P("pipe", None),
        P("pipe", None, "tensor"),
        P("pipe", None, "tensor"),
        P("pipe", None, "tensor"),
        P("pipe", "tensor", None),
        P(),
        P(None, ("pipe", "tensor")),
    )
    out_specs = (P("dp", ("pipe", "tensor")), P("dp"))
    return jax.shard_map(
        per_device, mesh=mesh, in_specs=in_specs, out_specs=out_specs, check_vma=False
    )
```

time: 448 us -> 117 us (0.26); the launches traced: 441 us -> 116 us
  waiting for transfers between devices: 173 us -> 0 us
  matrix products: 139 us -> 0 us
  Pallas kernels: 0 us -> 113 us
  blocking collectives: 54 us -> 0 us
  starting transfers between devices: 22.3 us -> 0 us
  local copies, waits for them, and re-layouts: 20.2 us -> 2.63 us
  other arithmetic: 17 us -> 0 us
  between operations: 14.7 us -> 0.65 us
    dot_general x45 -> x0, matrix products: 137 us -> none  [the longest x7 42.4 us: project(): query = jnp.dot(segment, layer_query, preferred_element_type=jnp.float32)]
    pallas_call x0 -> x1, Pallas kernels: none -> 113 us  [per_device(): pl.pallas_call(functools.partial(relay_kernel, dims), out_shape=(jax.Shap...]
    reduce_scatter x7 -> x0, waiting for transfers between devices: 70.4 us -> none  [per_device(): lax.psum_scatter(jnp.dot(context, layer_out, preferred_element_type=jnp.f...]
    psum x1 -> x0, waiting for transfers between devices: 54.3 us -> none  [broadcast(): return lax.psum(kept, axis)]
    ppermute x6 -> x0, waiting for transfers between devices: 36 us -> none  [passed_along(): return lax.ppermute(value, axis, pairs)]
    psum x2 -> x0, blocking collectives: 23.6 us -> none  [per_device(): exp_total, target = lax.psum((exp_local, target_local), ('pipe', 'tensor'))]
    ppermute x6 -> x0, starting transfers between devices: 21.8 us -> none  [passed_along(): return lax.ppermute(value, axis, pairs)]
    dot_general x2 -> x0, local copies, waits for them, and re-layouts: 17.7 us -> none  [the longest x1 11.3 us: project(): query = jnp.dot(segment, layer_query, preferred_element_type=jnp.float32)]
  transfers between devices with their start and end apart: 15 -> 0, of which waited for: 15 -> 0; matrix products, arithmetic and copies ran while one was open for 0% -> 0% of each run, Pallas kernels for 0% -> 0%
where the time goes in v1:
time: 117 us; the launch traced here: 116 us
  Pallas kernels  113 us (97%)
  local copies, waits for them, and re-layouts  2.63 us (2%)
    pallas_call x1, Pallas kernels, per_device(): pl.pallas_call(functools.partial(relay_kernel, dims), out_shape=(jax.Shap...  113 us

profile of v1, /device:TPU:0, one launch (start us, length us, event | category | flops | bytes accessed | tf_op | source)
XLA Modules:
  0.0 116.3 jit_solution(13737254682882716988)
XLA Ops:
  0.6 113.1 %shard_map.122 = (f32[4,64]{1,0:T(4,128)}, f32[8,128]{1,0:T(8,128)}) custom-call(bf16[4,32,4096]{2,1,0:T(8,128)(2,1)} %embeds_ref.1, s32[4,64]{1,0:T(4,128)} %labels_ref.1, f32[1,4096]{1,0:T(1,128)} %gain_ref.1, bf16[1,4096,1024]{2,1,0:T(8,128)(2,1)} %w_query_ref.1, bf16[1,4096,512]{2,1,0:T(8,128)(2,1)} %w_key_ref.1, bf16[1,4096,512]{2,1,0:T(8,128)(2,1)} %w_value_ref.1, ...), custom_call_target="tpu_custom_call" | custom-call | tf_op jit(solution)/shard_map/pallas_call | solution.py:428
  113.7 1.3 %constant_dynamic-slice_fusion = f32[4,8]{1,0:T(4,128)} fusion(f32[4,64]{1,0:T(4,128)} %get-tuple-element.4, s32[]{:T(128)S(6)} %select_n.3), kind=kLoop, calls=%fused_computation.1 | loop fusion | bytes 260 | tf_op jit(solution)/shard_map/dynamic_slice | solution.py:473
  115.0 1.3 %slice_reduce_fusion = f32[4]{0:T(128)} fusion(f32[8,128]{1,0:T(8,128)} %get-tuple-element.5), kind=kLoop, calls=%fused_computation | loop fusion | bytes 32 | tf_op jit(solution)/shard_map/slice | solution.py:474

commit v2 on v1

v2 whole, which is shorter than its diff:
```python
import functools
import math

import jax
import jax.numpy as jnp
import numpy as np
from jax import lax
from jax.experimental import pallas as pl
from jax.experimental.pallas import tpu as pltpu
from jax.sharding import PartitionSpec as P

HD = 128
EPSILON = 1e-05
ROPE_BASE = 500000.0
LANES = 128
MESH = pl.DeviceIdType.MESH
NEG = -1e30


def round_up(value, step):
    return (value + step - 1) // step * step


def rotary_tables(seq_len):
    half = HD // 2
    inverse = (ROPE_BASE ** (-2.0 * np.arange(half, dtype=np.float64) / HD)).astype(np.float32)
    angles = (np.arange(seq_len, dtype=np.float32)[:, None] * inverse[None, :]).astype(np.float64)
    cosine, sine = np.cos(angles), np.sin(angles)
    cos_table = np.concatenate([cosine, cosine], axis=1).astype(np.float32)
    sin_table = np.concatenate([-sine, sine], axis=1).astype(np.float32)
    return cos_table, sin_table


def relay_kernel(
    dims,
    embeds_ref, labels_ref, gain_ref, w_query_ref, w_key_ref, w_value_ref, w_out_ref,
    final_gain_ref, head_ref, cos_ref, sin_ref,
    loss_ref, score_ref,
    wqkv, wout, whead, full, acc, ctx, part, rs, outst, fin, logits, ghid,
    labcol, slab, stats, tots,
    w_sem, wo_sem, wh_sem, e_sem,
    in_send, in_recv, g_send, g_recv, r_send, r_recv,
    h_send, h_recv, s_send, s_recv, t_send, t_recv, u_send, u_recv,
):
    n_pipe, n_tensor, micro, rows, width, heads_q, heads_kv, vocab_dev, lag_in, lag_out = dims
    group = n_pipe * n_tensor
    seq_len = rows * n_tensor
    q_width, kv_width = heads_q * HD, heads_kv * HD
    per_kv = heads_q // heads_kv
    n_chunk, _, chunk = wout.shape
    last = n_pipe - 1
    p = lax.axis_index("pipe")
    t = lax.axis_index("tensor")
    slot = p * n_tensor + t
    near = [n_pipe - 2, n_pipe - 3] if n_pipe >= 3 else list(range(last))
    far = [q for q in range(last) if q not in near]

    def cols(n):
        return pl.ds(pl.multiple_of(n * chunk, chunk), chunk)

    def w_copies(n):
        q_at, k_at = q_width, q_width + kv_width
        pieces = ((w_query_ref, 0, q_at), (w_key_ref, q_at, k_at), (w_value_ref, k_at, k_at + kv_width))
        return [
            pltpu.make_async_copy(
                ref.at[0, cols(n), :], wqkv.at[n, :, pl.ds(lo, hi - lo)], w_sem.at[n, i]
            )
            for i, (ref, lo, hi) in enumerate(pieces)
        ]

    def wo_copy(n):
        return pltpu.make_async_copy(w_out_ref.at[0, :, cols(n)], wout.at[n], wo_sem.at[n])

    def e_copy(m, n):
        return pltpu.make_async_copy(embeds_ref.at[m, :, cols(n)], full.at[m, n, t], e_sem.at[m, n])

    head_copy = pltpu.make_async_copy(head_ref, whead, wh_sem)

    @pl.when(p == 0)
    def _():
        for m in range(micro):
            for n in range(n_chunk):
                e_copy(m, n).start()

    for n in range(n_chunk):
        for copy in w_copies(n):
            copy.start()

    @pl.when(p > 0)
    def _():
        for n in range(n_chunk):
            wo_copy(n).start()
        head_copy.start()

    def ring(j):
        peer = lax.rem(slot + j, group)
        return peer, {"pipe": peer // n_tensor, "tensor": lax.rem(peer, n_tensor)}

    barrier = pltpu.get_barrier_semaphore()
    for j in range(1, group):
        pl.semaphore_signal(barrier, inc=1, device_id=ring(j)[1], device_id_type=MESH)
    pl.semaphore_wait(barrier, group - 1)

    def remote(src, dst, send, recv, device):
        return pltpu.make_async_remote_copy(
            src_ref=src, dst_ref=dst, send_sem=send, recv_sem=recv,
            device_id=device, device_id_type=MESH,
        )

    def mate(j):
        return lax.rem(t + j, n_tensor)

    def in_copy(m, n):
        return remote(outst.at[m, n], full.at[m, n, t], in_send.at[m, n], in_recv.at[m, n],
                      {"pipe": lax.rem(p + 1, n_pipe)})

    def g_copy(m, n, j):
        return remote(full.at[m, n, t], full.at[m, n, t], g_send.at[m, n, j], g_recv.at[m, n, t],
                      {"tensor": mate(j)})

    def g_arrival(m, n, j):
        who = mate(j)
        return remote(full.at[m, n, who], full.at[m, n, who], g_send.at[m, n, j],
                      g_recv.at[m, n, who], {"tensor": who})

    def r_copy(m, n, j):
        who = mate(j)
        return remote(part.at[m, n, who], rs.at[m, n, t], r_send.at[m, n, j],
                      r_recv.at[m, n, t], {"tensor": who})

    def r_arrival(m, n, j):
        who = mate(j)
        return remote(part.at[m, n, who], rs.at[m, n, who], r_send.at[m, n, j],
                      r_recv.at[m, n, who], {"tensor": who})

    def h_copy(m, n, k, to):
        piece = fin.at[m, n, t]
        return remote(piece, piece, h_send.at[m, n, k], h_recv.at[m, n], {"pipe": to})

    def s_copy(m, n, j):
        return remote(fin.at[m, n, t], fin.at[m, n, t], s_send.at[m, n, j], s_recv.at[m, n, t],
                      {"tensor": mate(j)})

    def s_arrival(m, n, j):
        who = mate(j)
        return remote(fin.at[m, n, who], fin.at[m, n, who], s_send.at[m, n, j],
                      s_recv.at[m, n, who], {"tensor": who})

    def scaled(squares):
        return lax.rsqrt(squares * (1.0 / width) + EPSILON)

    row_at = lax.broadcasted_iota(jnp.int32, (per_kv * seq_len, seq_len), 0)
    key_at = lax.broadcasted_iota(jnp.int32, (per_kv * seq_len, seq_len), 1)
    causal = lax.rem(row_at, seq_len) >= key_at
    no_squares = jnp.zeros((seq_len, 1), jnp.float32)

    def layer(m, carry):
        def arrive(n):
            @pl.when(p > 0)
            def _():
                in_copy(m, n).wait_recv()

            @pl.when(p == 0)
            def _():
                e_copy(m, n).wait()

            for j in range(1, n_tensor):
                g_copy(m, n, j).start()

        acc[...] = jnp.zeros_like(acc)
        for n in range(lag_in):
            arrive(n)

        def project(n, squares):
            @pl.when(n + lag_in < n_chunk)
            def _():
                arrive(n + lag_in)

            for j in range(1, n_tensor):
                g_arrival(m, n, j).wait_recv()

            @pl.when(m == 0)
            def _():
                for copy in w_copies(n):
                    copy.wait()

            @pl.when((m == 0) & (p == 0) & (n == n_chunk - 2))
            def _():
                for i in range(n_chunk):
                    wo_copy(i).start()

            wide = full[m, n].astype(jnp.float32).reshape(seq_len, chunk)
            lhs = (wide * gain_ref[:, cols(n)]).astype(jnp.bfloat16)
            for at in range(0, q_width + 2 * kv_width, kv_width):
                acc[:, at : at + kv_width] += jnp.dot(
                    lhs, wqkv[n, :, at : at + kv_width], preferred_element_type=jnp.float32
                )
            return squares + jnp.sum(wide * wide, axis=-1, keepdims=True)

        factor = scaled(lax.fori_loop(0, n_chunk, project, no_squares))

        @pl.when((m == 0) & (p == 0))
        def _():
            head_copy.start()

        cosine, sine = cos_ref[...] * factor, sin_ref[...] * factor

        def turned(at):
            one = acc[:, at : at + HD]
            return (one * cosine + pltpu.roll(one, HD // 2, 1) * sine).astype(jnp.bfloat16)

        for h in range(heads_kv):
            queries = [turned((h * per_kv + g) * HD) for g in range(per_kv)]
            query = jnp.concatenate(queries, axis=0) if per_kv > 1 else queries[0]
            key = turned(q_width + h * HD)
            v_at = q_width + kv_width + h * HD
            value = (acc[:, v_at : v_at + HD] * factor).astype(jnp.bfloat16)
            scores = lax.dot_general(
                query, key, (((1,), (1,)), ((), ())), preferred_element_type=jnp.float32
            ) * (1.0 / math.sqrt(HD))
            scores = jnp.where(causal, scores, NEG)
            shifted = jnp.exp(scores - jnp.max(scores, axis=-1, keepdims=True))
            probs = (shifted / jnp.sum(shifted, axis=-1, keepdims=True)).astype(jnp.bfloat16)
            context = jnp.dot(probs, value, preferred_element_type=jnp.float32)
            for g in range(per_kv):
                at = (h * per_kv + g) * HD
                ctx[:, at : at + HD] = context[g * seq_len : (g + 1) * seq_len].astype(jnp.bfloat16)

        def combine(n):
            block = part[m, n, t].astype(jnp.float32)
            for j in range(1, n_tensor):
                r_arrival(m, n, j).wait_recv()
                block += rs[m, n, mate(j)].astype(jnp.float32)
            state = (full[m, n, t].astype(jnp.float32) + block).astype(jnp.bfloat16)

            @pl.when(p < last)
            def _():
                outst[m, n] = state
                in_copy(m, n).start()

            @pl.when(p == last)
            def _():
                fin[m, n, t] = state
                for k, to in enumerate(near):
                    h_copy(m, n, k, to).start()

        def output(n, c):
            @pl.when(m == 0)
            def _():
                wo_copy(n).wait()

            product = jnp.dot(ctx[...], wout[n], preferred_element_type=jnp.float32)
            part[m, n] = product.reshape(n_tensor, rows, chunk).astype(jnp.bfloat16)
            for j in range(1, n_tensor):
                r_copy(m, n, j).start()

            @pl.when(n >= lag_out)
            def _():
                combine(n - lag_out)

            return c

        lax.fori_loop(0, n_chunk, output, 0)
        for n in range(n_chunk - lag_out, n_chunk):
            combine(n)
        return carry

    lax.fori_loop(0, micro, layer, 0)

    pad = jnp.zeros((LANES - micro, seq_len), jnp.float32)
    labcol[...] = jnp.concatenate([labels_ref[...].astype(jnp.float32), pad], axis=0).T
    slab[...] = jnp.zeros_like(slab)
    lane = lax.broadcasted_iota(jnp.int32, (seq_len, LANES), 1)
    entry = (lax.broadcasted_iota(jnp.int32, (seq_len, vocab_dev), 1) + slot * vocab_dev).astype(
        jnp.float32
    )
    head_copy.wait()

    def head(m, carry):
        def arrive(n):
            @pl.when(p < last)
            def _():
                h_copy(m, n, 0, last).wait_recv()

            if far:
                for k in range(2):
                    @pl.when((p == near[k]) & (lax.rem(n, 2) == k))
                    def _():
                        for f, to in enumerate(far):
                            h_copy(m, n, f, to).start()

            for j in range(1, n_tensor):
                s_copy(m, n, j).start()

        logits[m] = jnp.zeros_like(logits[m])
        ghid[m] = jnp.zeros_like(ghid[m])
        for n in range(lag_in):
            arrive(n)

        def score(n, squares):
            @pl.when(n + lag_in < n_chunk)
            def _():
                arrive(n + lag_in)

            for j in range(1, n_tensor):
                s_arrival(m, n, j).wait_recv()
            wide = fin[m, n].astype(jnp.float32).reshape(seq_len, chunk)
            lhs = (wide * final_gain_ref[:, cols(n)]).astype(jnp.bfloat16)
            logits[m] += jnp.dot(lhs, whead[cols(n), :], preferred_element_type=jnp.float32)
            ghid[m] += lax.dot_general(
                lhs, lhs, (((1,), (1,)), ((), ())), preferred_element_type=jnp.float32
            )
            return squares + jnp.sum(wide * wide, axis=-1, keepdims=True)

        factor = scaled(lax.fori_loop(0, n_chunk, score, no_squares))
        local = logits[m] * factor
        logits[m] = local
        own = jnp.sum(jnp.where(lane == m, labcol[...], 0.0), axis=-1, keepdims=True)
        peak = jnp.max(local, axis=-1, keepdims=True)
        mass = jnp.sum(jnp.exp(local - peak), axis=-1, keepdims=True)
        target = jnp.sum(jnp.where(entry == own, local, 0.0), axis=-1, keepdims=True)
        kept = slab[...]
        for i, column in enumerate((peak, mass, target, factor)):
            kept = jnp.where(lane == i * micro + m, column, kept)
        slab[...] = kept
        return carry

    lax.fori_loop(0, micro, head, 0)

    n_stats = stats.shape[1]
    slab_cols = slab[...]
    stats[slot] = slab_cols.T[:n_stats]

    def exchange(buffer, send, recv):
        def copy(j):
            peer, device = ring(j)
            return remote(buffer.at[slot], buffer.at[slot], send.at[j], recv.at[slot], device)

        def arrival(j):
            peer, device = ring(j)
            return remote(buffer.at[peer], buffer.at[peer], send.at[j], recv.at[peer], device)

        for j in range(1, group):
            copy(j).start()
        for j in range(1, group):
            arrival(j).wait_recv()
        return copy

    stats_copy = exchange(stats, t_send, t_recv)
    peaks = stats[:, :micro, :]
    peak_row = jnp.max(peaks, axis=0)
    masses = jnp.exp(peaks - peak_row[None]) * stats[:, micro : 2 * micro, :]
    log_norm = peak_row + jnp.log(jnp.sum(masses, axis=0))
    loss_ref[...] = log_norm - jnp.sum(stats[:, 2 * micro : 3 * micro, :], axis=0)
    factor_rows = stats[0, 3 * micro : 4 * micro, :]
    labels_t = labcol[...]
    norm_t = jnp.concatenate([log_norm, pad], axis=0).T

    tot_rows = tots.shape[1]
    row_id = lax.broadcasted_iota(jnp.int32, (tot_rows, seq_len), 0)
    sums = jnp.zeros((tot_rows, seq_len), jnp.float32)
    for m in range(micro):
        onehot = (entry == labels_t[:, m : m + 1]).astype(jnp.float32)
        errors = (jnp.exp(logits[m] - norm_t[:, m : m + 1]) - onehot).astype(jnp.bfloat16)
        gram = lax.dot_general(
            errors, errors, (((1,), (1,)), ((), ())), preferred_element_type=jnp.float32
        )
        f_at = 3 * micro + m
        weighted = gram * ghid[m] * slab_cols[:, f_at : f_at + 1]
        row = jnp.sum(weighted, axis=0, keepdims=True) * factor_rows[m : m + 1]
        sums = jnp.where(row_id == m, row, sums)
    tots[slot] = sums
    tots_copy = exchange(tots, u_send, u_recv)
    total = jnp.sum(jnp.sum(tots[...], axis=0), axis=-1, keepdims=True)
    score_ref[...] = jnp.broadcast_to(jnp.sqrt(total) / seq_len, score_ref.shape)

    def drain(m, carry):
        for n in range(n_chunk):
            for j in range(1, n_tensor):
                g_copy(m, n, j).wait_send()
                s_copy(m, n, j).wait_send()
                r_copy(m, n, j).wait_send()

        @pl.when(p < last)
        def _():
            for n in range(n_chunk):
                in_copy(m, n).wait_send()

        @pl.when(p == last)
        def _():
            for n in range(n_chunk):
                for k, to in enumerate(near):
                    h_copy(m, n, k, to).wait_send()

        if far:
            for k in range(2):
                @pl.when(p == near[k])
                def _():
                    for n in range(k, n_chunk, 2):
                        for f, to in enumerate(far):
                            h_copy(m, n, f, to).wait_send()

        return carry

    lax.fori_loop(0, micro, drain, 0)
    for j in range(1, group):
        stats_copy(j).wait_send()
        tots_copy(j).wait_send()


def per_device(embeds, labels, norm_gain, w_query, w_key, w_value, w_out, final_gain, head_weight):
    n_pipe = lax.axis_size("pipe")
    n_tensor = lax.axis_size("tensor")
    group = n_pipe * n_tensor
    micro, rows, width = embeds.shape
    seq_len = rows * n_tensor
    heads_q = w_query.shape[2] // HD
    heads_kv = w_key.shape[2] // HD
    qkv_width = (heads_q + 2 * heads_kv) * HD
    depth = w_out.shape[1]
    vocab_dev = head_weight.shape[1]
    n_chunk, lag_in, lag_out = 4, 1, 2
    chunk = width // n_chunk
    n_far = max(n_pipe, 2)
    cos_table, sin_table = rotary_tables(seq_len)
    dims = (n_pipe, n_tensor, micro, rows, width, heads_q, heads_kv, vocab_dev, lag_in, lag_out)
    bf16, f32 = jnp.bfloat16, jnp.float32
    dma = pltpu.SemaphoreType.DMA
    any_spec = pl.BlockSpec(memory_space=pl.ANY)
    vmem_spec = pl.BlockSpec(memory_space=pltpu.VMEM)
    stat_rows = round_up(4 * micro, 8)
    tot_rows = round_up(micro, 8)
    losses, scores = pl.pallas_call(
        functools.partial(relay_kernel, dims),
        out_shape=(
            jax.ShapeDtypeStruct((micro, seq_len), f32),
            jax.ShapeDtypeStruct((tot_rows, LANES), f32),
        ),
        in_specs=[any_spec, vmem_spec, vmem_spec] + [any_spec] * 4
        + [vmem_spec, any_spec, vmem_spec, vmem_spec],
        out_specs=(vmem_spec, vmem_spec),
        scratch_shapes=[
            pltpu.VMEM((n_chunk, chunk, qkv_width), bf16),
            pltpu.VMEM((n_chunk, depth, chunk), bf16),
            pltpu.VMEM((width, vocab_dev), bf16),
            pltpu.VMEM((micro, n_chunk, n_tensor, rows, chunk), bf16),
            pltpu.VMEM((seq_len, qkv_width), f32),
            pltpu.VMEM((seq_len, depth), bf16),
            pltpu.VMEM((micro, n_chunk, n_tensor, rows, chunk), bf16),
            pltpu.VMEM((micro, n_chunk, n_tensor, rows, chunk), bf16),
            pltpu.VMEM((micro, n_chunk, rows, chunk), bf16),
            pltpu.VMEM((micro, n_chunk, n_tensor, rows, chunk), bf16),
            pltpu.VMEM((micro, seq_len, vocab_dev), f32),
            pltpu.VMEM((micro, seq_len, seq_len), f32),
            pltpu.VMEM((seq_len, LANES), f32),
            pltpu.VMEM((seq_len, LANES), f32),
            pltpu.VMEM((group, stat_rows, seq_len), f32),
            pltpu.VMEM((group, tot_rows, seq_len), f32),
            dma((n_chunk, 3)), dma((n_chunk,)), dma, dma((micro, n_chunk)),
            dma((micro, n_chunk)), dma((micro, n_chunk)),
            dma((micro, n_chunk, n_tensor)), dma((micro, n_chunk, n_tensor)),
            dma((micro, n_chunk, n_tensor)), dma((micro, n_chunk, n_tensor)),
            dma((micro, n_chunk, n_far)), dma((micro, n_chunk)),
            dma((micro, n_chunk, n_tensor)), dma((micro, n_chunk, n_tensor)),
            dma((group,)), dma((group,)), dma((group,)), dma((group,)),
        ],
        compiler_params=pltpu.CompilerParams(
            collective_id=0, has_side_effects=True, vmem_limit_bytes=58 * 1024 * 1024
        ),
    )(
        embeds, labels, norm_gain, w_query, w_key, w_value, w_out,
        final_gain.reshape(1, width), head_weight, jnp.asarray(cos_table), jnp.asarray(sin_table),
    )
    loss_width = seq_len // group
    device_slot = lax.axis_index("pipe") * n_tensor + lax.axis_index("tensor")
    token_loss = lax.dynamic_slice_in_dim(losses, device_slot * loss_width, loss_width, 1)
    return (token_loss, scores[:micro, 0])


def solution(mesh):
    in_specs = (
        P("dp", "tensor", None),
        P("dp", None),
        P("pipe", None),
        P("pipe", None, "tensor"),
        P("pipe", None, "tensor"),
        P("pipe", None, "tensor"),
        P("pipe", "tensor", None),
        P(),
        P(None, ("pipe", "tensor")),
    )
    out_specs = (P("dp", ("pipe", "tensor")), P("dp"))
    return jax.shard_map(
        per_device, mesh=mesh, in_specs=in_specs, out_specs=out_specs, check_vma=False
    )
```

time: 117 us -> 103 us (0.88)
  Pallas kernels: 113 us -> 99.7 us
    pallas_call x1, Pallas kernels: 113 us -> 99.7 us  [per_device(): pl.pallas_call(functools.partial(relay_kernel, dims), out_shape=(jax.Shap...]
where the time goes in v2:
time: 103 us
  Pallas kernels  99.7 us (97%)
  local copies, waits for them, and re-layouts  2.63 us (3%)
    pallas_call x1, Pallas kernels, per_device(): pl.pallas_call(functools.partial(relay_kernel, dims), out_shape=(jax.Shap...  99.7 us

profile of v2, /device:TPU:0, one launch (start us, length us, event | category | flops | bytes accessed | tf_op | source)
XLA Modules:
  0.0 102.9 jit_solution(1215636837796394806)
XLA Ops:
  0.6 99.7 %shard_map.122 = (f32[4,64]{1,0:T(4,128)}, f32[8,128]{1,0:T(8,128)}) custom-call(bf16[4,32,4096]{2,1,0:T(8,128)(2,1)} %embeds_ref.1, s32[4,64]{1,0:T(4,128)} %labels_ref.1, f32[1,4096]{1,0:T(1,128)} %gain_ref.1, bf16[1,4096,1024]{2,1,0:T(8,128)(2,1)} %w_query_ref.1, bf16[1,4096,512]{2,1,0:T(8,128)(2,1)} %w_key_ref.1, bf16[1,4096,512]{2,1,0:T(8,128)(2,1)} %w_value_ref.1, ...), custom_call_target="tpu_custom_call" | custom-call | tf_op jit(solution)/shard_map/pallas_call | solution.py:433
  100.3 1.3 %constant_dynamic-slice_fusion = f32[4,8]{1,0:T(4,128)} fusion(f32[4,64]{1,0:T(4,128)} %get-tuple-element.4, s32[]{:T(128)S(6)} %select_n.3), kind=kLoop, calls=%fused_computation.1 | loop fusion | bytes 260 | tf_op jit(solution)/shard_map/dynamic_slice | solution.py:476
  101.6 1.3 %slice_reduce_fusion = f32[4]{0:T(128)} fusion(f32[8,128]{1,0:T(8,128)} %get-tuple-element.5), kind=kLoop, calls=%fused_computation | loop fusion | bytes 32 | tf_op jit(solution)/shard_map/slice | solution.py:477

commit v3 on v2

--- a/solution.py
+++ b/solution.py
@@ -42,9 +42,11 @@
     in_send, in_recv, g_send, g_recv, r_send, r_recv,
     h_send, h_recv, s_send, s_recv, t_send, t_recv, u_send, u_recv,
 ):
-    n_pipe, n_tensor, micro, rows, width, heads_q, heads_kv, vocab_dev, lag_in, lag_out = dims
+    n_pipe, n_tensor, micro, batch, own_rows, width, heads_q, heads_kv, vocab_dev, lag_in, lag_out = dims
     group = n_pipe * n_tensor
-    seq_len = rows * n_tensor
+    rows = batch * own_rows
+    seq_len = own_rows * n_tensor
+    step_len = rows * n_tensor
     q_width, kv_width = heads_q * HD, heads_kv * HD
     per_kv = heads_q // heads_kv
     n_chunk, _, chunk = wout.shape
@@ -152,7 +154,7 @@
     row_at = lax.broadcasted_iota(jnp.int32, (per_kv * seq_len, seq_len), 0)
     key_at = lax.broadcasted_iota(jnp.int32, (per_kv * seq_len, seq_len), 1)
     causal = lax.rem(row_at, seq_len) >= key_at
-    no_squares = jnp.zeros((seq_len, 1), jnp.float32)
+    no_squares = jnp.zeros((step_len, 1), jnp.float32)
 
     def layer(m, carry):
         def arrive(n):
@@ -189,7 +191,7 @@
                 for i in range(n_chunk):
                     wo_copy(i).start()
 
-            wide = full[m, n].astype(jnp.float32).reshape(seq_len, chunk)
+            wide = full[m, n].astype(jnp.float32).reshape(step_len, chunk)
             lhs = (wide * gain_ref[:, cols(n)]).astype(jnp.bfloat16)
             for at in range(0, q_width + 2 * kv_width, kv_width):
                 acc[:, at : at + kv_width] += jnp.dot(
@@ -203,28 +205,46 @@
         def _():
             head_copy.start()
 
-        cosine, sine = cos_ref[...] * factor, sin_ref[...] * factor
-
-        def turned(at):
-            one = acc[:, at : at + HD]
-            return (one * cosine + pltpu.roll(one, HD // 2, 1) * sine).astype(jnp.bfloat16)
-
-        for h in range(heads_kv):
-            queries = [turned((h * per_kv + g) * HD) for g in range(per_kv)]
-            query = jnp.concatenate(queries, axis=0) if per_kv > 1 else queries[0]
-            key = turned(q_width + h * HD)
-            v_at = q_width + kv_width + h * HD
-            value = (acc[:, v_at : v_at + HD] * factor).astype(jnp.bfloat16)
-            scores = lax.dot_general(
-                query, key, (((1,), (1,)), ((), ())), preferred_element_type=jnp.float32
-            ) * (1.0 / math.sqrt(HD))
-            scores = jnp.where(causal, scores, NEG)
-            shifted = jnp.exp(scores - jnp.max(scores, axis=-1, keepdims=True))
-            probs = (shifted / jnp.sum(shifted, axis=-1, keepdims=True)).astype(jnp.bfloat16)
-            context = jnp.dot(probs, value, preferred_element_type=jnp.float32)
-            for g in range(per_kv):
-                at = (h * per_kv + g) * HD
-                ctx[:, at : at + HD] = context[g * seq_len : (g + 1) * seq_len].astype(jnp.bfloat16)
+        def of_sequence(value, b):
+            starts = [i * rows + b * own_rows for i in range(n_tensor)]
+            return jnp.concatenate([value[at : at + own_rows] for at in starts], axis=0)
+
+        def attend(b):
+            own_factor = of_sequence(factor, b)
+            cosine, sine = cos_ref[...] * own_factor, sin_ref[...] * own_factor
+
+            def head_of(at):
+                starts = [i * rows + b * own_rows for i in range(n_tensor)]
+                return jnp.concatenate(
+                    [acc[lo : lo + own_rows, at : at + HD] for lo in starts], axis=0
+                )
+
+            def turned(at):
+                one = head_of(at)
+                return (one * cosine + pltpu.roll(one, HD // 2, 1) * sine).astype(jnp.bfloat16)
+
+            for h in range(heads_kv):
+                queries = [turned((h * per_kv + g) * HD) for g in range(per_kv)]
+                query = jnp.concatenate(queries, axis=0) if per_kv > 1 else queries[0]
+                key = turned(q_width + h * HD)
+                value = (head_of(q_width + kv_width + h * HD) * own_factor).astype(jnp.bfloat16)
+                scores = lax.dot_general(
+                    query, key, (((1,), (1,)), ((), ())), preferred_element_type=jnp.float32
+                ) * (1.0 / math.sqrt(HD))
+                scores = jnp.where(causal, scores, NEG)
+                shifted = jnp.exp(scores - jnp.max(scores, axis=-1, keepdims=True))
+                probs = (shifted / jnp.sum(shifted, axis=-1, keepdims=True)).astype(jnp.bfloat16)
+                context = jnp.dot(probs, value, preferred_element_type=jnp.float32)
+                for g in range(per_kv):
+                    at = (h * per_kv + g) * HD
+                    for i in range(n_tensor):
+                        lo, frm = i * rows + b * own_rows, g * seq_len + i * own_rows
+                        ctx[lo : lo + own_rows, at : at + HD] = context[
+                            frm : frm + own_rows
+                        ].astype(jnp.bfloat16)
+
+        for b in range(batch):
+            attend(b)
 
         def combine(n):
             block = part[m, n, t].astype(jnp.float32)
@@ -267,11 +287,21 @@
 
     lax.fori_loop(0, micro, layer, 0)
 
-    pad = jnp.zeros((LANES - micro, seq_len), jnp.float32)
-    labcol[...] = jnp.concatenate([labels_ref[...].astype(jnp.float32), pad], axis=0).T
+    lab_pad = jnp.zeros((LANES - micro * batch, seq_len), jnp.float32)
+    lab = jnp.concatenate([labels_ref[...].astype(jnp.float32), lab_pad], axis=0).T
+    few = lax.broadcasted_iota(jnp.int32, (own_rows, LANES), 1)
+    for i in range(n_tensor):
+        for b in range(batch):
+            block = jnp.zeros((own_rows, LANES), jnp.float32)
+            for m in range(micro):
+                at = m * batch + b
+                column = lab[i * own_rows : (i + 1) * own_rows, at : at + 1]
+                block = jnp.where(few == m, column, block)
+            lo = i * rows + b * own_rows
+            labcol[lo : lo + own_rows, :] = block
     slab[...] = jnp.zeros_like(slab)
-    lane = lax.broadcasted_iota(jnp.int32, (seq_len, LANES), 1)
-    entry = (lax.broadcasted_iota(jnp.int32, (seq_len, vocab_dev), 1) + slot * vocab_dev).astype(
+    lane = lax.broadcasted_iota(jnp.int32, (step_len, LANES), 1)
+    entry = (lax.broadcasted_iota(jnp.int32, (step_len, vocab_dev), 1) + slot * vocab_dev).astype(
         jnp.float32
     )
     head_copy.wait()
@@ -304,7 +334,7 @@
 
             for j in range(1, n_tensor):
                 s_arrival(m, n, j).wait_recv()
-            wide = fin[m, n].astype(jnp.float32).reshape(seq_len, chunk)
+            wide = fin[m, n].astype(jnp.float32).reshape(step_len, chunk)
             lhs = (wide * final_gain_ref[:, cols(n)]).astype(jnp.bfloat16)
             logits[m] += jnp.dot(lhs, whead[cols(n), :], preferred_element_type=jnp.float32)
             ghid[m] += lax.dot_general(
@@ -354,11 +384,18 @@
     loss_ref[...] = log_norm - jnp.sum(stats[:, 2 * micro : 3 * micro, :], axis=0)
     factor_rows = stats[0, 3 * micro : 4 * micro, :]
     labels_t = labcol[...]
+    pad = jnp.zeros((LANES - micro, step_len), jnp.float32)
     norm_t = jnp.concatenate([log_norm, pad], axis=0).T
 
+    def sequence_at(shape, dim):
+        return lax.rem(lax.div(lax.broadcasted_iota(jnp.int32, shape, dim), own_rows), batch)
+
+    square = (step_len, step_len)
+    same = sequence_at(square, 0) == sequence_at(square, 1)
+
     tot_rows = tots.shape[1]
-    row_id = lax.broadcasted_iota(jnp.int32, (tot_rows, seq_len), 0)
-    sums = jnp.zeros((tot_rows, seq_len), jnp.float32)
+    row_id = lax.broadcasted_iota(jnp.int32, (tot_rows, step_len), 0)
+    sums = jnp.zeros((tot_rows, step_len), jnp.float32)
     for m in range(micro):
         onehot = (entry == labels_t[:, m : m + 1]).astype(jnp.float32)
         errors = (jnp.exp(logits[m] - norm_t[:, m : m + 1]) - onehot).astype(jnp.bfloat16)
@@ -366,13 +403,19 @@
             errors, errors, (((1,), (1,)), ((), ())), preferred_element_type=jnp.float32
         )
         f_at = 3 * micro + m
-        weighted = gram * ghid[m] * slab_cols[:, f_at : f_at + 1]
+        weighted = jnp.where(same, gram * ghid[m] * slab_cols[:, f_at : f_at + 1], 0.0)
         row = jnp.sum(weighted, axis=0, keepdims=True) * factor_rows[m : m + 1]
         sums = jnp.where(row_id == m, row, sums)
     tots[slot] = sums
     tots_copy = exchange(tots, u_send, u_recv)
-    total = jnp.sum(jnp.sum(tots[...], axis=0), axis=-1, keepdims=True)
-    score_ref[...] = jnp.broadcast_to(jnp.sqrt(total) / seq_len, score_ref.shape)
+    total = jnp.sum(tots[...], axis=0)
+    of_row = sequence_at((tot_rows, step_len), 1)
+    out_lane = lax.broadcasted_iota(jnp.int32, score_ref.shape, 1)
+    scored = jnp.zeros(score_ref.shape, jnp.float32)
+    for b in range(batch):
+        own = jnp.sum(jnp.where(of_row == b, total, 0.0), axis=-1, keepdims=True)
+        scored = jnp.where(out_lane == b, jnp.sqrt(own) / seq_len, scored)
+    score_ref[...] = scored
 
     def drain(m, carry):
         for n in range(n_chunk):
@@ -412,18 +455,21 @@
     n_pipe = lax.axis_size("pipe")
     n_tensor = lax.axis_size("tensor")
     group = n_pipe * n_tensor
-    micro, rows, width = embeds.shape
-    seq_len = rows * n_tensor
+    sequences, own_rows, width = embeds.shape
+    seq_len = own_rows * n_tensor
+    batch = 2 if sequences % 2 == 0 else 1
+    micro, rows = sequences // batch, batch * own_rows
+    step_len = rows * n_tensor
     heads_q = w_query.shape[2] // HD
     heads_kv = w_key.shape[2] // HD
     qkv_width = (heads_q + 2 * heads_kv) * HD
     depth = w_out.shape[1]
     vocab_dev = head_weight.shape[1]
-    n_chunk, lag_in, lag_out = 4, 1, 2
+    n_chunk, lag_in, lag_out = 8, 2, 3
     chunk = width // n_chunk
     n_far = max(n_pipe, 2)
     cos_table, sin_table = rotary_tables(seq_len)
-    dims = (n_pipe, n_tensor, micro, rows, width, heads_q, heads_kv, vocab_dev, lag_in, lag_out)
+    dims = (n_pipe, n_tensor, micro, batch, own_rows, width, heads_q, heads_kv, vocab_dev, lag_in, lag_out)
     bf16, f32 = jnp.bfloat16, jnp.float32
     dma = pltpu.SemaphoreType.DMA
     any_spec = pl.BlockSpec(memory_space=pl.ANY)
@@ -433,7 +479,7 @@
     losses, scores = pl.pallas_call(
         functools.partial(relay_kernel, dims),
         out_shape=(
-            jax.ShapeDtypeStruct((micro, seq_len), f32),
+            jax.ShapeDtypeStruct((micro, step_len), f32),
             jax.ShapeDtypeStruct((tot_rows, LANES), f32),
         ),
         in_specs=[any_spec, vmem_spec, vmem_spec] + [any_spec] * 4
@@ -444,18 +490,18 @@
             pltpu.VMEM((n_chunk, depth, chunk), bf16),
             pltpu.VMEM((width, vocab_dev), bf16),
             pltpu.VMEM((micro, n_chunk, n_tensor, rows, chunk), bf16),
-            pltpu.VMEM((seq_len, qkv_width), f32),
-            pltpu.VMEM((seq_len, depth), bf16),
+            pltpu.VMEM((step_len, qkv_width), f32),
+            pltpu.VMEM((step_len, depth), bf16),
             pltpu.VMEM((micro, n_chunk, n_tensor, rows, chunk), bf16),
             pltpu.VMEM((micro, n_chunk, n_tensor, rows, chunk), bf16),
             pltpu.VMEM((micro, n_chunk, rows, chunk), bf16),
             pltpu.VMEM((micro, n_chunk, n_tensor, rows, chunk), bf16),
-            pltpu.VMEM((micro, seq_len, vocab_dev), f32),
-            pltpu.VMEM((micro, seq_len, seq_len), f32),
-            pltpu.VMEM((seq_len, LANES), f32),
-            pltpu.VMEM((seq_len, LANES), f32),
-            pltpu.VMEM((group, stat_rows, seq_len), f32),
-            pltpu.VMEM((group, tot_rows, seq_len), f32),
+            pltpu.VMEM((micro, step_len, vocab_dev), f32),
+            pltpu.VMEM((micro, step_len, step_len), f32),
+            pltpu.VMEM((step_len, LANES), f32),
+            pltpu.VMEM((step_len, LANES), f32),
+            pltpu.VMEM((group, stat_rows, step_len), f32),
+            pltpu.VMEM((group, tot_rows, step_len), f32),
             dma((n_chunk, 3)), dma((n_chunk,)), dma, dma((micro, n_chunk)),
             dma((micro, n_chunk)), dma((micro, n_chunk)),
             dma((micro, n_chunk, n_tensor)), dma((micro, n_chunk, n_tensor)),
@@ -468,13 +514,15 @@
             collective_id=0, has_side_effects=True, vmem_limit_bytes=58 * 1024 * 1024
         ),
     )(
-        embeds, labels, norm_gain, w_query, w_key, w_value, w_out,
+        embeds.reshape(micro, rows, width), labels, norm_gain, w_query, w_key, w_value, w_out,
         final_gain.reshape(1, width), head_weight, jnp.asarray(cos_table), jnp.asarray(sin_table),
     )
     loss_width = seq_len // group
     device_slot = lax.axis_index("pipe") * n_tensor + lax.axis_index("tensor")
+    losses = losses.reshape(micro, n_tensor, batch, own_rows).transpose(0, 2, 1, 3)
+    losses = losses.reshape(sequences, seq_len)
     token_loss = lax.dynamic_slice_in_dim(losses, device_slot * loss_width, loss_width, 1)
-    return (token_loss, scores[:micro, 0])
+    return (token_loss, scores[:micro, :batch].reshape(sequences))
 
 
 def solution(mesh):

time: 103 us -> 109 us (1.058)
  Pallas kernels: 99.7 us -> 105 us
    pallas_call x1, Pallas kernels: 99.7 us -> 105 us  [per_device(): pl.pallas_call(functools.partial(relay_kernel, dims), out_shape=(jax.Shap...]
    reshape x0 -> x3, local copies, waits for them, and re-layouts: none -> 1.41 us  [the longest x1 0.73 us: per_device(): losses.reshape(micro, n_tensor, batch, own_rows).transpose(0, 2, 1, 3)]
where the time goes in v3:
time: 109 us
  Pallas kernels  105 us (96%)
  local copies, waits for them, and re-layouts  2.74 us (3%)
    pallas_call x1, Pallas kernels, per_device(): pl.pallas_call(functools.partial(relay_kernel, dims), out_shape=(jax.Shap...  105 us

profile of v3, /device:TPU:0, one launch (start us, length us, event | category | flops | bytes accessed | tf_op | source)
XLA Modules:
  0.0 108.6 jit_solution(3927808362454717320)
XLA Ops:
  0.6 105.2 %shard_map.122 = (f32[2,128]{1,0:T(2,128)}, f32[8,128]{1,0:T(8,128)}) custom-call(bf16[2,64,4096]{2,1,0:T(8,128)(2,1)} %bitcast.3, s32[4,64]{1,0:T(4,128)} %labels_ref.1, f32[1,4096]{1,0:T(1,128)} %gain_ref.1, bf16[1,4096,1024]{2,1,0:T(8,128)(2,1)} %w_query_ref.1, bf16[1,4096,512]{2,1,0:T(8,128)(2,1)} %w_key_ref.1, bf16[1,4096,512]{2,1,0:T(8,128)(2,1)} %w_value_ref.1, ...), custom_call_target="tpu_custom_call" | custom-call | tf_op jit(solution)/shard_map/pallas_call | solution.py:479
  105.9 0.7 slice.3
  106.5 0.6 reshape.23
  107.1 0.7 reshape.21
  107.9 0.1 reshape.22
  108.0 0.7 constant_dynamic-slice_fusion
  (1 shorter events, 0.0 us)

commit v4 on v3

--- a/solution.py
+++ b/solution.py
@@ -457,7 +457,7 @@
     group = n_pipe * n_tensor
     sequences, own_rows, width = embeds.shape
     seq_len = own_rows * n_tensor
-    batch = 2 if sequences % 2 == 0 else 1
+    batch = 1
     micro, rows = sequences // batch, batch * own_rows
     step_len = rows * n_tensor
     heads_q = w_query.shape[2] // HD
@@ -465,7 +465,7 @@
     qkv_width = (heads_q + 2 * heads_kv) * HD
     depth = w_out.shape[1]
     vocab_dev = head_weight.shape[1]
-    n_chunk, lag_in, lag_out = 8, 2, 3
+    n_chunk, lag_in, lag_out = 8, 2, 2
     chunk = width // n_chunk
     n_far = max(n_pipe, 2)
     cos_table, sin_table = rotary_tables(seq_len)

time: 109 us -> 114 us (1.046)
  Pallas kernels: 105 us -> 110 us
    pallas_call x1, Pallas kernels: 105 us -> 110 us  [per_device(): pl.pallas_call(functools.partial(relay_kernel, dims), out_shape=(jax.Shap...]
    reshape x3 -> x0, local copies, waits for them, and re-layouts: 1.41 us -> none  [the longest x1 0.73 us: per_device(): losses.reshape(micro, n_tensor, batch, own_rows).transpose(0, 2, 1, 3)]
where the time goes in v4:
time: 114 us
  Pallas kernels  110 us (96%)
  local copies, waits for them, and re-layouts  2.63 us (2%)
    pallas_call x1, Pallas kernels, per_device(): pl.pallas_call(functools.partial(relay_kernel, dims), out_shape=(jax.Shap...  110 us

profile of v4, /device:TPU:0, one launch (start us, length us, event | category | flops | bytes accessed | tf_op | source)
XLA Modules:
  0.0 113.6 jit_solution(1050402284975285686)
XLA Ops:
  0.6 110.4 %shard_map.122 = (f32[4,64]{1,0:T(4,128)}, f32[8,128]{1,0:T(8,128)}) custom-call(bf16[4,32,4096]{2,1,0:T(8,128)(2,1)} %embeds_ref.1, s32[4,64]{1,0:T(4,128)} %labels_ref.1, f32[1,4096]{1,0:T(1,128)} %gain_ref.1, bf16[1,4096,1024]{2,1,0:T(8,128)(2,1)} %w_query_ref.1, bf16[1,4096,512]{2,1,0:T(8,128)(2,1)} %w_key_ref.1, bf16[1,4096,512]{2,1,0:T(8,128)(2,1)} %w_value_ref.1, ...), custom_call_target="tpu_custom_call" | custom-call | tf_op jit(solution)/shard_map/pallas_call | solution.py:479
  111.0 1.3 %constant_dynamic-slice_fusion = f32[4,8]{1,0:T(4,128)} fusion(f32[4,64]{1,0:T(4,128)} %get-tuple-element.4, s32[]{:T(128)S(6)} %select_n.3), kind=kLoop, calls=%fused_computation.1 | loop fusion | bytes 260 | tf_op jit(solution)/shard_map/dynamic_slice | solution.py:524
  112.3 1.3 %slice_reduce_fusion = f32[4]{0:T(128)} fusion(f32[8,128]{1,0:T(8,128)} %get-tuple-element.5), kind=kLoop, calls=%fused_computation | loop fusion | bytes 32 | tf_op jit(solution)/shard_map/slice | solution.py:525
